TPU v7x, 512 devices: a whole 4x4x16 slice. The times are simulated.
512 devices in a mesh: seq: 64 (over y, z), dp: 8 (over x, core).
Axes of the slice: x: 4, y: 4, z: 16, core: 2. Of those that a mesh axis runs over, the one named last changes fastest.
Arguments:
- inputs: bfloat16 [8, 8192, 256], P('dp', 'seq'), may hold values from -6 to 6
- cotangent: bfloat16 [8, 8192, 256], P('dp', 'seq'), may hold values from -6 to 6
- filter_taps: float32 [8192, 256], P('seq'), may hold values from -3 to 3
- skip_gain: float32 [256], replicated, may hold values from -1 to 1
Outputs:
- outputs: bfloat16 [8, 8192, 256], P('dp', 'seq')
- filter_grad: float32 [8192, 256], P('seq', 'dp')
All inputs are finite; a program needn't handle non-finite values.
Results may differ from a plain program's by a relative error of at most 0.001.
Values sent between devices are 32-bit elements; how exact they have to be, the bound alone decides.
No kernel may reach another device: no remote copies, remote signals or barrier semaphores. Data moves between devices by JAX's collectives and lax.ppermute only.
A program may use at most 64 MiB of HBM per device.

v0:
```python
import math

import jax
import jax.numpy as jnp
import numpy as np
from jax import lax
from jax.sharding import PartitionSpec as P


def contract(form, left, right):
    return jnp.einsum(
        form, left, right, precision=lax.Precision.HIGHEST, preferred_element_type=jnp.float32
    )


def complex_times(left, right):
    return jnp.stack(
        [left[0] * right[0] - left[1] * right[1], left[0] * right[1] + left[1] * right[0]]
    )


def complex_table(form, values, cosine, sine):
    real_part = contract(form, values[0], cosine) - contract(form, values[1], sine)
    imag_part = contract(form, values[0], sine) + contract(form, values[1], cosine)
    return jnp.stack([real_part, imag_part])


def static_phase(product, period, direction):
    angle = direction * 2.0 * math.pi * (product % period) / period
    return (jnp.asarray(np.cos(angle), jnp.float32), jnp.asarray(np.sin(angle), jnp.float32))


def traced_phase(product, period, direction):
    angle = (product % period).astype(jnp.float32) * (direction * 2.0 * math.pi / period)
    return jnp.stack([jnp.cos(angle), jnp.sin(angle)])


def slot_order(parts):
    order = np.arange(parts)
    return order


def forward_spectrum(values):
    batch_count, row_count, chan_count = values.shape
    parts = lax.axis_size("seq")
    own_index = lax.axis_index("seq")
    group_size = row_count // parts
    period = 2 * row_count * parts
    blocks = values.reshape(batch_count, parts, group_size, chan_count)
    columns = lax.all_to_all(blocks, "seq", split_axis=1, concat_axis=1, tiled=True)
    offsets = own_index * group_size + jnp.arange(group_size, dtype=jnp.int32)
    slots = slot_order(parts)
    freq_first = np.concatenate([2 * slots, 2 * slots + 1])
    cosine, sine = static_phase(np.outer(np.arange(parts), freq_first), 2 * parts, -1.0)
    spectrum = jnp.stack(
        [contract("kqac,ql->klac", columns, cosine), contract("kqac,ql->klac", columns, sine)]
    )
    twiddle = traced_phase(
        jnp.asarray(freq_first, jnp.int32)[:, None] * offsets[None, :], period, -1.0
    )
    spectrum = complex_times(spectrum, twiddle[:, None, :, :, None])
    spectrum = spectrum.reshape(2, batch_count, 2, parts, group_size, chan_count)
    spectrum = lax.all_to_all(spectrum, "seq", split_axis=3, concat_axis=3, tiled=True)
    lanes = spectrum.shape[2]
    spectrum = spectrum.reshape(2, batch_count, lanes, row_count, chan_count)
    local_index = np.arange(row_count)
    cosine, sine = static_phase(np.outer(local_index, local_index), row_count, -1.0)
    return complex_table("kemc,mn->kenc", spectrum, cosine, sine)


def inverse_rows(spectrum):
    batch_count = spectrum.shape[1]
    row_count = spectrum.shape[3]
    chan_count = spectrum.shape[4]
    parts = lax.axis_size("seq")
    own_index = lax.axis_index("seq")
    group_size = row_count // parts
    period = 2 * row_count * parts
    local_index = np.arange(row_count)
    cosine, sine = static_phase(np.outer(local_index, local_index), row_count, 1.0)
    mixed = complex_table("kenc,nm->kemc", spectrum, cosine, sine)
    blocks = mixed.reshape(2, batch_count, 2, parts, group_size, chan_count)
    blocks = lax.all_to_all(blocks, "seq", split_axis=3, concat_axis=3, tiled=True)
    slots = np.arange(parts)
    freq_grid = np.stack([2 * slots, 2 * slots + 1])
    offsets = own_index * group_size + jnp.arange(group_size, dtype=jnp.int32)
    twiddle = traced_phase(
        jnp.asarray(freq_grid, jnp.int32)[:, :, None] * offsets[None, None, :], period, 1.0
    )
    turned = complex_times(blocks, twiddle[:, None, :, :, :, None])
    cosine, sine = static_phase(
        freq_grid[:, :, None] * np.arange(parts)[None, None, :], 2 * parts, 1.0
    )
    summed = contract("kesac,esq->kqac", turned[0], cosine) - contract(
        "kesac,esq->kqac", turned[1], sine
    )
    settled = lax.all_to_all(summed, "seq", split_axis=1, concat_axis=1, tiled=True)
    return settled.reshape(batch_count, row_count, chan_count) / period


def body(inputs, cotangent, filter_taps, skip_gain):
    sample_count = inputs.shape[0]
    signal = inputs.astype(jnp.float32)
    grads = cotangent.astype(jnp.float32)
    joined = forward_spectrum(jnp.concatenate([signal, grads], axis=0))
    sig_spec = joined[:, :sample_count]
    grad_spec = joined[:, sample_count:]
    filt_spec = forward_spectrum(filter_taps[None])
    product = complex_times(sig_spec, filt_spec)
    conjugate = jnp.stack([sig_spec[0], -sig_spec[1]])
    cross = jnp.sum(complex_times(grad_spec, conjugate), axis=1, keepdims=True)
    conv = inverse_rows(product)
    outputs = (conv + skip_gain * signal).astype(jnp.bfloat16)
    shares = lax.psum_scatter(cross, "dp", scatter_dimension=4, tiled=True)
    filter_grad = inverse_rows(shares)[0]
    return (outputs, filter_grad)


def solution(mesh):
    placed = (P("dp", "seq", None), P("dp", "seq", None), P("seq", None), P())
    return jax.shard_map(
        body,
        mesh=mesh,
        in_specs=placed,
        out_specs=(P("dp", "seq", None), P("seq", "dp")),
        check_vma=False,
    )
```

profile of v0, /device:TPU:6, one launch (start us, length us, event | category | flops | bytes accessed | tf_op | source)
XLA Modules:
  0.0 321.6 jit_solution(4126093902371951826)
XLA Ops:
  7.2 1.6 reshape_broadcast_in_dim.3
  8.8 18.9 %all-to-all-start.2 = ((f32[1,64,2,256]{3,2,0,1:T(2,128)}), f32[1,64,2,256]{3,2,0,1:T(2,128)S(1)}, u32[]{:S(2)}, u32[]{:S(2)}) async-start(f32[1,64,2,256]{3,2,0,1:T(2,128)} %bitcast.19), calls=%async_computation.2 | async-start | bytes 262144 | tf_op jit(solution)/shard_map/all_to_all | solution.py:50
  28.8 0.8 copy.131
  29.6 14.4 %all-to-all-done.2 = f32[1,64,2,256]{3,2,0,1:T(2,128)S(1)} async-done(((f32[1,64,2,256]{3,2,0,1:T(2,128)}), f32[1,64,2,256]{3,2,0,1:T(2,128)S(1)}, u32[]{:S(2)}, u32[]{:S(2)}) %all-to-all-start.2) | async-done | bytes 131104 | tf_op jit(solution)/shard_map/all_to_all | solution.py:50
  44.0 5.7 %all-to-all-start = ((f32[2,64,2,256]{3,2,0,1:T(2,128)}), f32[2,64,2,256]{3,2,0,1:T(2,128)S(1)}, u32[]{:S(2)}, u32[]{:S(2)}) async-start(f32[2,64,2,256]{3,2,0,1:T(2,128)} %copy.131), calls=%async_computation | async-start | bytes 524288 | tf_op jit(solution)/shard_map/all_to_all | solution.py:50
  52.2 1.0 pad_maximum_fusion.1
  53.2 17.2 %all-to-all-done = f32[2,64,2,256]{3,2,0,1:T(2,128)S(1)} async-done(((f32[2,64,2,256]{3,2,0,1:T(2,128)}), f32[2,64,2,256]{3,2,0,1:T(2,128)S(1)}, u32[]{:S(2)}, u32[]{:S(2)}) %all-to-all-start) | async-done | bytes 262176 | tf_op jit(solution)/shard_map/all_to_all | solution.py:50
  70.4 6.4 %all-to-all-start.3 = ((f32[2,1,2,64,2,256]{5,2,4,1,0,3:T(2,128)}), f32[2,1,2,64,2,256]{5,2,4,1,0,3:T(2,128)S(1)}, u32[]{:S(2)}, u32[]{:S(2)}) async-start(f32[2,1,2,64,2,256]{5,2,4,1,0,3:T(2,128)} %pad_maximum_fusion.1), calls=%async_computation.3 | async-start | bytes 1048576 | tf_op jit(solution)/shard_map/all_to_all | solution.py:63
  79.2 1.5 pad_maximum_fusion
  80.7 26.7 %all-to-all-done.3 = f32[2,1,2,64,2,256]{5,2,4,1,0,3:T(2,128)S(1)} async-done(((f32[2,1,2,64,2,256]{5,2,4,1,0,3:T(2,128)}), f32[2,1,2,64,2,256]{5,2,4,1,0,3:T(2,128)S(1)}, u32[]{:S(2)}, u32[]{:S(2)}) %all-to-all-start.3) | async-done | bytes 524320 | tf_op jit(solution)/shard_map/all_to_all | solution.py:63
  107.4 7.1 %all-to-all-start.1 = ((f32[2,2,2,64,2,256]{5,2,4,1,0,3:T(2,128)}), f32[2,2,2,64,2,256]{5,2,4,1,0,3:T(2,128)S(1)}, u32[]{:S(2)}, u32[]{:S(2)}) async-start(f32[2,2,2,64,2,256]{5,2,4,1,0,3:T(2,128)} %pad_maximum_fusion), calls=%async_computation.1 | async-start | bytes 2097152 | tf_op jit(solution)/shard_map/all_to_all | solution.py:63
  116.1 51.9 %all-to-all-done.1 = f32[2,2,2,64,2,256]{5,2,4,1,0,3:T(2,128)S(1)} async-done(((f32[2,2,2,64,2,256]{5,2,4,1,0,3:T(2,128)}), f32[2,2,2,64,2,256]{5,2,4,1,0,3:T(2,128)S(1)}, u32[]{:S(2)}, u32[]{:S(2)}) %all-to-all-start.1) | async-done | bytes 1048608 | tf_op jit(solution)/shard_map/all_to_all | solution.py:63
  177.2 24.2 %reduce-scatter.2.cloned.1.call-done = f32[2,1,2,128,32]{3,4,2,1,0:T(8,128)} async-done(((f32[2,1,2,128,256]{3,4,2,1,0:T(8,128)}), f32[2,1,2,128,32]{3,4,2,1,0:T(8,128)}) %reduce-scatter.2.cloned.1.call-update) | async-done | bytes 65552 | tf_op jit(solution)/shard_map/reduce_scatter | solution.py:114
  201.4 1.0 fusion.33
  203.4 0.9 reshape.437
  204.3 15.6 %all-to-all-start.6 = ((f32[64,1,256]{2,1,0:T(1,128)}), f32[64,1,256]{2,1,0:T(1,128)S(1)}, u32[]{:S(2)}, u32[]{:S(2)}) async-start(f32[64,1,256]{2,1,0:T(1,128)} %reshape.437), calls=%async_computation.7 | async-start | bytes 131072 | tf_op jit(solution)/shard_map/all_to_all | solution.py:83
  220.6 1.0 pad_maximum_fusion.2
  221.6 13.3 %all-to-all-done.6 = f32[64,1,256]{2,1,0:T(1,128)S(1)} async-done(((f32[64,1,256]{2,1,0:T(1,128)}), f32[64,1,256]{2,1,0:T(1,128)S(1)}, u32[]{:S(2)}, u32[]{:S(2)}) %all-to-all-start.6) | async-done | bytes 65568 | tf_op jit(solution)/shard_map/all_to_all | solution.py:83
  235.0 5.5 %all-to-all-start.4 = ((f32[2,1,2,64,2,256]{5,2,4,1,0,3:T(2,128)}), f32[2,1,2,64,2,256]{5,2,4,1,0,3:T(2,128)S(1)}, u32[]{:S(2)}, u32[]{:S(2)}) async-start(f32[2,1,2,64,2,256]{5,2,4,1,0,3:T(2,128)} %pad_maximum_fusion.2), calls=%async_computation.4 | async-start | bytes 1048576 | tf_op jit(solution)/shard_map/all_to_all | solution.py:83
  245.4 26.8 %all-to-all-done.4 = f32[2,1,2,64,2,256]{5,2,4,1,0,3:T(2,128)S(1)} async-done(((f32[2,1,2,64,2,256]{5,2,4,1,0,3:T(2,128)}), f32[2,1,2,64,2,256]{5,2,4,1,0,3:T(2,128)S(1)}, u32[]{:S(2)}, u32[]{:S(2)}) %all-to-all-start.4) | async-done | bytes 524320 | tf_op jit(solution)/shard_map/all_to_all | solution.py:83
  272.2 6.6 %all-to-all-start.7 = ((f32[1,64,2,32]{3,2,0,1:T(2,128)}), f32[1,64,2,32]{3,2,0,1:T(2,128)S(1)}, u32[]{:S(2)}, u32[]{:S(2)}) async-start(f32[1,64,2,32]{3,2,0,1:T(2,128)} %copy.177), calls=%async_computation.8 | async-start | bytes 131072 | tf_op jit(solution)/shard_map/all_to_all | solution.py:97
  280.6 13.0 %all-to-all-done.7 = f32[1,64,2,32]{3,2,0,1:T(2,128)S(1)} async-done(((f32[1,64,2,32]{3,2,0,1:T(2,128)}), f32[1,64,2,32]{3,2,0,1:T(2,128)S(1)}, u32[]{:S(2)}, u32[]{:S(2)}) %all-to-all-start.7) | async-done | bytes 16416 | tf_op jit(solution)/shard_map/all_to_all | solution.py:97
  293.5 4.6 %all-to-all-start.5 = ((f32[1,64,2,256]{3,2,0,1:T(2,128)}), f32[1,64,2,256]{3,2,0,1:T(2,128)S(1)}, u32[]{:S(2)}, u32[]{:S(2)}) async-start(f32[1,64,2,256]{3,2,0,1:T(2,128)} %copy.163), calls=%async_computation.5 | async-start | bytes 262144 | tf_op jit(solution)/shard_map/all_to_all | solution.py:97
  298.9 14.5 %all-to-all-done.5 = f32[1,64,2,256]{3,2,0,1:T(2,128)S(1)} async-done(((f32[1,64,2,256]{3,2,0,1:T(2,128)}), f32[1,64,2,256]{3,2,0,1:T(2,128)S(1)}, u32[]{:S(2)}, u32[]{:S(2)}) %all-to-all-start.5) | async-done | bytes 131104 | tf_op jit(solution)/shard_map/all_to_all | solution.py:97
  (101 shorter events, 26.6 us)
Async XLA Ops:
  8.8 18.9 %copy-start.5 = (bf16[1,128,256]{2,1,0:T(8,128)(2,1)S(1)}, bf16[1,128,256]{2,1,0:T(8,128)(2,1)}, u32[]{:S(2)}) copy-start(bf16[1,128,256]{2,1,0:T(8,128)(2,1)} %param.24) | copy-start | bytes 196612
  8.8 35.2 %all-to-all-start.2 = ((f32[1,64,2,256]{3,2,0,1:T(2,128)}), f32[1,64,2,256]{3,2,0,1:T(2,128)S(1)}, u32[]{:S(2)}, u32[]{:S(2)}) async-start(f32[1,64,2,256]{3,2,0,1:T(2,128)} %bitcast.19), calls=%async_computation.2 | async-start | bytes 262144 | tf_op jit(solution)/shard_map/all_to_all | solution.py:50
  27.7 0.8 copy-start.9
  44.0 6.5 %copy-start.12 = (f32[64,128,1]{1,0,2:T(8,128)S(1)}, f32[64,128,1]{1,0,2:T(8,128)}, u32[]{:S(2)}) copy-start(f32[64,128,1]{1,0,2:T(8,128)} %constant.84) | copy-start | bytes 98308
  44.0 26.4 %all-to-all-start = ((f32[2,64,2,256]{3,2,0,1:T(2,128)}), f32[2,64,2,256]{3,2,0,1:T(2,128)S(1)}, u32[]{:S(2)}, u32[]{:S(2)}) async-start(f32[2,64,2,256]{3,2,0,1:T(2,128)} %copy.131), calls=%async_computation | async-start | bytes 524288 | tf_op jit(solution)/shard_map/all_to_all | solution.py:50
  50.5 0.8 copy-start.13
  53.2 23.6 %copy-start.11 = (f32[64,128,1,1]{1,0,3,2:T(8,128)S(1)}, f32[64,128,1,1]{1,0,3,2:T(8,128)}, u32[]{:S(2)}) copy-start(f32[64,128,1,1]{1,0,3,2:T(8,128)} %constant.80) | copy-start | bytes 98308
  70.4 37.0 %all-to-all-start.3 = ((f32[2,1,2,64,2,256]{5,2,4,1,0,3:T(2,128)}), f32[2,1,2,64,2,256]{5,2,4,1,0,3:T(2,128)S(1)}, u32[]{:S(2)}, u32[]{:S(2)}) async-start(f32[2,1,2,64,2,256]{5,2,4,1,0,3:T(2,128)} %pad_maximum_fusion.1), calls=%async_computation.3 | async-start | bytes 1048576 | tf_op jit(solution)/shard_map/all_to_all | solution.py:63
  76.9 0.8 copy-start.10
  107.4 60.6 %all-to-all-start.1 = ((f32[2,2,2,64,2,256]{5,2,4,1,0,3:T(2,128)}), f32[2,2,2,64,2,256]{5,2,4,1,0,3:T(2,128)S(1)}, u32[]{:S(2)}, u32[]{:S(2)}) async-start(f32[2,2,2,64,2,256]{5,2,4,1,0,3:T(2,128)} %pad_maximum_fusion), calls=%async_computation.1 | async-start | bytes 2097152 | tf_op jit(solution)/shard_map/all_to_all | solution.py:63
  114.5 86.9 %reduce-scatter.2.cloned.1.call-start = ((), (), s32[]{:S(2)}) async-start(), calls=%async_computation.9 | async-start | bytes 589824 | tf_op jit(solution)/shard_map/reduce_scatter | solution.py:114
  114.9 0.8 copy-start.8
  168.9 0.8 copy-start.3
  169.7 0.8 copy-start.4
  173.2 0.8 copy-start
  175.3 0.8 copy-start.1
  201.4 1.0 copy-start.7
  204.3 30.6 %all-to-all-start.6 = ((f32[64,1,256]{2,1,0:T(1,128)}), f32[64,1,256]{2,1,0:T(1,128)S(1)}, u32[]{:S(2)}, u32[]{:S(2)}) async-start(f32[64,1,256]{2,1,0:T(1,128)} %reshape.437), calls=%async_computation.7 | async-start | bytes 131072 | tf_op jit(solution)/shard_map/all_to_all | solution.py:83
  221.6 18.8 %copy-start.15 = (s32[2,64]{1,0:T(2,128)S(1)}, s32[2,64]{1,0:T(2,128)}, u32[]{:S(2)}) copy-start(s32[2,64]{1,0:T(2,128)} %constant.75.clone) | copy-start | bytes 1540
  235.0 37.2 %all-to-all-start.4 = ((f32[2,1,2,64,2,256]{5,2,4,1,0,3:T(2,128)}), f32[2,1,2,64,2,256]{5,2,4,1,0,3:T(2,128)S(1)}, u32[]{:S(2)}, u32[]{:S(2)}) async-start(f32[2,1,2,64,2,256]{5,2,4,1,0,3:T(2,128)} %pad_maximum_fusion.2), calls=%async_computation.4 | async-start | bytes 1048576 | tf_op jit(solution)/shard_map/all_to_all | solution.py:83
  242.6 0.8 copy-start.2
  243.5 0.8 copy-start.6
  272.2 21.3 %all-to-all-start.7 = ((f32[1,64,2,32]{3,2,0,1:T(2,128)}), f32[1,64,2,32]{3,2,0,1:T(2,128)S(1)}, u32[]{:S(2)}, u32[]{:S(2)}) async-start(f32[1,64,2,32]{3,2,0,1:T(2,128)} %copy.177), calls=%async_computation.8 | async-start | bytes 131072 | tf_op jit(solution)/shard_map/all_to_all | solution.py:97
  293.5 19.8 %all-to-all-start.5 = ((f32[1,64,2,256]{3,2,0,1:T(2,128)}), f32[1,64,2,256]{3,2,0,1:T(2,128)S(1)}, u32[]{:S(2)}, u32[]{:S(2)}) async-start(f32[1,64,2,256]{3,2,0,1:T(2,128)} %copy.163), calls=%async_computation.5 | async-start | bytes 262144 | tf_op jit(solution)/shard_map/all_to_all | solution.py:97
  (2 other events, 1.3 us)
Sparse Core Ops, SparseCore 0:
  173.3 27.9 reduce-scatter.1
where the time goes:
time: 323 us; the launch traced here: 322 us
  waiting for transfers between devices  202 us (63%)
  starting transfers between devices  70.6 us (22%)
  local copies, waits for them, and re-layouts  16.6 us (5%)
  between operations  14.6 us (5%)
  matrix products  10.7 us (3%)
  other arithmetic  7.12 us (2%)
    all_to_all x2, waiting for transfers between devices, forward_spectrum(): lax.all_to_all(spectrum, 'seq', split_axis=3, concat_axis=3, tiled=True)  78.6 us
    all_to_all x2, waiting for transfers between devices, inverse_rows(): lax.all_to_all(blocks, 'seq', split_axis=3, concat_axis=3, tiled=True)  40.1 us
    all_to_all x2, waiting for transfers between devices, forward_spectrum(): lax.all_to_all(blocks, 'seq', split_axis=1, concat_axis=1, tiled=True)  31.6 us
    all_to_all x2, waiting for transfers between devices, inverse_rows(): lax.all_to_all(summed, 'seq', split_axis=1, concat_axis=1, tiled=True)  27.5 us
    all_to_all x2, starting transfers between devices, forward_spectrum(): lax.all_to_all(blocks, 'seq', split_axis=1, concat_axis=1, tiled=True)  24.5 us
    reduce_scatter x1, waiting for transfers between devices, body(): shares = lax.psum_scatter(cross, 'dp', scatter_dimension=4, tiled=True)  24.2 us
    all_to_all x2, starting transfers between devices, inverse_rows(): lax.all_to_all(blocks, 'seq', split_axis=3, concat_axis=3, tiled=True)  21.1 us
    all_to_all x2, starting transfers between devices, forward_spectrum(): lax.all_to_all(spectrum, 'seq', split_axis=3, concat_axis=3, tiled=True)  13.5 us
  transfers between devices with their start and end apart: 9, of which 9 were waited for; matrix products, arithmetic and copies ran while one was open for 6% of the time, Pallas kernels for 0%

commit v1 on v0

v1 whole, which is shorter than its diff:
```python
import functools
import math

import jax
import jax.numpy as jnp
import ml_dtypes
import numpy as np
from jax import lax
from jax.experimental import pallas as pl
from jax.experimental.pallas import tpu as pltpu
from jax.sharding import PartitionSpec as P

SIDE = 128
HALF = 64
TOTAL = SIDE * SIDE
GROUP = 4
BF = jnp.bfloat16
F32 = jnp.float32


def halves(table):
    high = table.astype(ml_dtypes.bfloat16)
    low = (table - high.astype(np.float64)).astype(ml_dtypes.bfloat16)
    return high, low


def tables():
    blocks = np.arange(HALF)
    places = np.arange(SIDE)
    outer = 2.0 * math.pi * np.outer(np.arange(HALF) + 0.5, blocks) / SIDE
    first = np.concatenate([np.cos(outer), -np.sin(outer)], axis=0)
    high, low = halves(first)
    first_in = np.concatenate([high, low, high, low], axis=1)
    last = first.T * (2.0 / TOTAL)
    high, low = halves(last)
    last_out = np.concatenate([high, high, low], axis=1)
    angle = 2.0 * math.pi * np.outer(np.arange(HALF) + 0.5, places) / TOTAL
    turn = np.stack([np.cos(angle), -np.sin(angle)]).astype(np.float32)
    inner = 2.0 * math.pi * (np.outer(places, places) % SIDE) / SIDE
    cosine, sine = np.cos(inner), np.sin(inner)
    forward = np.block([[cosine, -sine], [sine, cosine]])
    inverse = np.block([[cosine, sine], [-sine, cosine]])
    high, low = halves(forward)
    forward = np.concatenate([high, high, low], axis=0)
    high, low = halves(inverse)
    inverse = np.concatenate([high, high, low], axis=0)
    return first_in, last_out, turn, forward, inverse


def split(value):
    high = value.astype(BF)
    return high, (value - high.astype(F32)).astype(BF)


def dot(left, right):
    return jnp.dot(left, right, preferred_element_type=F32)


def pack_kernel(signal_ref, grads_ref, taps_ref, out_ref):
    for kind, ref in enumerate((signal_ref, grads_ref, taps_ref)):
        turned = ref[...].astype(F32).T
        for sub in range(GROUP):
            rows = turned[HALF * sub : HALF * (sub + 1)]
            out_ref[pl.ds(GROUP * kind + sub, HALF, stride=3 * GROUP), :] = rows


def main_kernel(in_ref, first_ref, last_ref, turn_ref, forward_ref, inverse_ref, out_ref, spread, spectrum, mixed, back):
    stride = 3 * GROUP
    cosine, sine = turn_ref[0], turn_ref[1]

    def load(kind, sub):
        return in_ref[pl.ds(GROUP * kind + sub, HALF, stride=stride), :]

    def place(index, column):
        real, imag = column[:HALF], column[HALF:]
        real, imag = real * cosine - imag * sine, real * sine + imag * cosine
        rows = pl.ds(HALF * index, HALF)
        for part, value in enumerate((real, imag)):
            high, low = split(value)
            spread[rows, pl.ds(SIDE * part, SIDE)] = high
            spread[rows, pl.ds(2 * SIDE + SIDE * part, SIDE)] = low

    for sub in range(GROUP):
        pair = jnp.concatenate([load(0, sub), load(1, sub)], axis=1).astype(BF)
        both = dot(first_ref[:, :SIDE], jnp.concatenate([pair, pair], axis=0))
        place(sub, both[:, :SIDE])
        place(GROUP + sub, both[:, SIDE:])
    for sub in range(0, GROUP, 2):
        pair = jnp.concatenate([load(2, sub), load(2, sub + 1)], axis=1)
        high, low = split(pair)
        both = dot(first_ref[...], jnp.concatenate([high, high, low, low], axis=0))
        place(2 * GROUP + sub, both[:, :SIDE])
        place(2 * GROUP + sub + 1, both[:, SIDE:])

    spectrum[...] = dot(spread[...], forward_ref[: 4 * SIDE]) + dot(
        spread[:, : 2 * SIDE], forward_ref[4 * SIDE :]
    )

    for sub in range(GROUP):
        parts = []
        for kind in range(3):
            rows = pl.ds(HALF * (GROUP * kind + sub), HALF)
            parts.append((spectrum[rows, :SIDE], spectrum[rows, SIDE:]))
        (sig_r, sig_i), (grad_r, grad_i), (filt_r, filt_i) = parts
        products = (
            (sub, sig_r * filt_r - sig_i * filt_i, sig_r * filt_i + sig_i * filt_r),
            (GROUP + sub, grad_r * sig_r + grad_i * sig_i, grad_i * sig_r - grad_r * sig_i),
        )
        for index, real, imag in products:
            rows = pl.ds(HALF * index, HALF)
            for part, value in enumerate((real, imag)):
                high, low = split(value)
                mixed[rows, pl.ds(SIDE * part, SIDE)] = high
                mixed[rows, pl.ds(2 * SIDE + SIDE * part, SIDE)] = low

    back[...] = dot(mixed[...], inverse_ref[: 4 * SIDE]) + dot(
        mixed[:, : 2 * SIDE], inverse_ref[4 * SIDE :]
    )

    for index in range(0, 2 * GROUP, 2):
        stacks = []
        for one in (index, index + 1):
            rows = pl.ds(HALF * one, HALF)
            real, imag = back[rows, :SIDE], back[rows, SIDE:]
            value = jnp.concatenate(
                [real * cosine + imag * sine, imag * cosine - real * sine], axis=0
            )
            high, low = split(value)
            stacks.append(jnp.concatenate([high, low, high], axis=0))
        both = dot(last_ref[...], jnp.concatenate(stacks, axis=1))
        out_ref[pl.ds(index, HALF, stride=2 * GROUP), :] = both[:, :SIDE]
        out_ref[pl.ds(index + 1, HALF, stride=2 * GROUP), :] = both[:, SIDE:]


def pick_kernel(in_ref, out_ref):
    for sub in range(GROUP):
        rows = in_ref[pl.ds(GROUP + sub, HALF, stride=2 * GROUP), :]
        out_ref[pl.ds(HALF * sub, HALF), :] = rows


def finish_kernel(in_ref, signal_ref, gain_ref, out_ref):
    rows = [in_ref[pl.ds(sub, HALF, stride=2 * GROUP), :] for sub in range(GROUP)]
    conv = jnp.concatenate(rows, axis=0).T
    out_ref[...] = (conv + gain_ref[...] * signal_ref[...].astype(F32)).astype(BF)


def sum_kernel(in_ref, out_ref):
    out_ref[...] = jnp.sum(in_ref[...], axis=0).T


def call(kernel, shape, dtype, *args, flops=1000, scratch=()):
    size = math.prod(shape) * jnp.dtype(dtype).itemsize
    size += sum(math.prod(a.shape) * a.dtype.itemsize for a in args)
    return pl.pallas_call(
        kernel,
        out_shape=jax.ShapeDtypeStruct(shape, dtype),
        scratch_shapes=list(scratch),
        cost_estimate=pl.CostEstimate(flops=flops, bytes_accessed=size, transcendentals=0),
        compiler_params=pltpu.CompilerParams(vmem_limit_bytes=24 * 1024 * 1024),
    )(*args)


def body(inputs, cotangent, filter_taps, skip_gain):
    _, rows, chans = inputs.shape
    parts = lax.axis_size("seq")
    shares = lax.axis_size("dp")
    signal = inputs[0]
    packed = call(pack_kernel, (parts * 3 * GROUP, rows), F32, signal, cotangent[0], filter_taps)
    packed = packed.reshape(parts, 3, GROUP, rows)
    columns = lax.all_to_all(packed, "seq", split_axis=0, concat_axis=0, tiled=True)
    columns = columns.reshape(parts * 3 * GROUP, rows)
    wide = 2 * SIDE
    settled = call(
        main_kernel,
        (parts * 2 * GROUP, rows),
        F32,
        columns,
        *[jnp.asarray(t) for t in tables()],
        flops=800_000_000,
        scratch=(
            pltpu.VMEM((3 * GROUP * HALF, 2 * wide), BF),
            pltpu.VMEM((3 * GROUP * HALF, wide), F32),
            pltpu.VMEM((2 * GROUP * HALF, 2 * wide), BF),
            pltpu.VMEM((2 * GROUP * HALF, wide), F32),
        ),
    )
    settled = settled.reshape(parts, 2 * GROUP, rows)
    owned = lax.all_to_all(settled, "seq", split_axis=0, concat_axis=0, tiled=True)
    owned = owned.reshape(parts * 2 * GROUP, rows)
    partial = call(pick_kernel, (chans, rows), F32, owned).reshape(shares, chans // shares, rows)
    partial = lax.all_to_all(partial, "dp", split_axis=0, concat_axis=0, tiled=True)
    outputs = call(finish_kernel, (rows, chans), BF, owned, signal, skip_gain[None])
    filter_grad = call(sum_kernel, (rows, chans // shares), F32, partial)
    return outputs[None], filter_grad


def solution(mesh):
    placed = (P("dp", "seq", None), P("dp", "seq", None), P("seq", None), P())
    return jax.shard_map(
        body,
        mesh=mesh,
        in_specs=placed,
        out_specs=(P("dp", "seq", None), P("seq", "dp")),
        check_vma=False,
    )
```

time: 323 us -> 90 us (0.28)
  the two profiles are of different devices: /device:TPU:6 before, /device:TPU:1 now
where the time goes in v1:
time: 90 us; the launch traced here: 89.6 us
  blocking collectives  69.8 us (78%)
  starting transfers between devices  7.88 us (9%)
  local copies, waits for them, and re-layouts  3.96 us (4%)
  waiting for transfers between devices  3.86 us (4%)
  Pallas kernels  3.34 us (4%)
    all_to_all x1, blocking collectives, body(): lax.all_to_all(packed, 'seq', split_axis=0, concat_axis=0, tiled=True)  43.9 us
    all_to_all x1, blocking collectives, body(): lax.all_to_all(settled, 'seq', split_axis=0, concat_axis=0, tiled=True)  25.9 us
    all_to_all x1, starting transfers between devices, body(): lax.all_to_all(partial, 'dp', split_axis=0, concat_axis=0, tiled=True)  7.88 us
    unnamed x21, local copies, waits for them, and re-layouts  3.96 us
    all_to_all x1, waiting for transfers between devices, body(): lax.all_to_all(partial, 'dp', split_axis=0, concat_axis=0, tiled=True)  3.86 us
    pallas_call x5, Pallas kernels, call(): pl.pallas_call(kernel, out_shape=jax.ShapeDtypeStruct(shape, dtype), scra...  3.34 us
  transfers between devices with their start and end apart: 1, of which 1 were waited for; matrix products, arithmetic and copies ran while one was open for 0% of the time, Pallas kernels for 1%

profile of v1, /device:TPU:1, one launch (start us, length us, event | category | flops | bytes accessed | tf_op | source)
XLA Modules:
  0.0 89.6 jit_solution(596444000233929750)
XLA Ops:
  0.6 0.0 copy-start
  0.6 0.8 copy-done
  1.5 0.0 copy-start.2
  1.5 0.9 %copy-done.2 = f32[128,256]{1,0:T(8,128)S(1)} copy-done((f32[128,256]{1,0:T(8,128)S(1)}, f32[128,256]{1,0:T(8,128)}, u32[]{:S(2)}) %copy-start.2) | copy-done | bytes 131096
  2.4 0.8 copy-done.3
  3.2 0.1 shard_map.104
  3.4 0.0 copy-start.5
  3.4 0.0 copy-start.6
  3.4 43.9 %all_to_all.15 = f32[64,3,4,128]{3,2,1,0:T(4,128)S(1)} all-to-all(f32[64,3,4,128]{3,2,1,0:T(4,128)S(1)} %bitcast.11), channel_id=1, replica_groups=mesh['seq'=64,'dp'=8] {'seq'}, dimensions={0} | all-to-all | bytes 786432 | tf_op jit(solution)/shard_map/all_to_all | solution.py:170
  47.3 0.0 copy-done.7
  47.3 0.0 copy-done.8
  47.3 0.0 copy-done.9
  47.3 0.0 copy-done.5
  47.4 0.0 copy-done.6
  47.4 1.7 %shard_map.105 = f32[512,128]{1,0:T(8,128)S(1)} custom-call(f32[768,128]{1,0:T(8,128)S(1)} %bitcast.12, bf16[128,256]{1,0:T(8,128)(2,1)S(1)} %copy-done.8, bf16[64,384]{1,0:T(8,128)(2,1)S(1)} %copy-done.9, f32[2,64,128]{2,1,0:T(8,128)S(1)} %copy-done.7, bf16[768,256]{1,0:T(8,128)(2,1)S(1)} %copy-done.6, bf16[768,256]{1,0:T(8,128)(2,1)S(1)} %copy-done.5), custom_call_target="tpu_custom_call" | custom-call | flops 800000000 | bytes 1622016 | tf_op jit(solution)/shard_map/pallas_call | solution.py:154
  49.1 25.9 %all_to_all.16 = f32[64,8,128]{2,1,0:T(8,128)S(1)} all-to-all(f32[64,8,128]{2,1,0:T(8,128)S(1)} %bitcast.13), channel_id=1, replica_groups=mesh['seq'=64,'dp'=8] {'seq'}, dimensions={0} | all-to-all | bytes 524288 | tf_op jit(solution)/shard_map/all_to_all | solution.py:188
  75.0 0.7 shard_map.107
  75.6 7.9 %all-to-all-start.2 = ((f32[8,32,128]{2,1,0:T(8,128)}), f32[8,32,128]{2,1,0:T(8,128)S(1)}, u32[]{:S(2)}, u32[]{:S(2)}) async-start(f32[8,32,128]{2,1,0:T(8,128)} %bitcast.8), calls=%async_computation.2 | async-start | bytes 262144 | tf_op jit(solution)/shard_map/all_to_all | solution.py:191
  83.5 0.0 copy-done.1
  83.5 0.7 copy-done.4
  84.2 0.7 shard_map.106
  84.9 3.9 %all-to-all-done.2.in_ref = f32[8,32,128]{2,1,0:T(8,128)S(1)} async-done(((f32[8,32,128]{2,1,0:T(8,128)}), f32[8,32,128]{2,1,0:T(8,128)S(1)}, u32[]{:S(2)}, u32[]{:S(2)}) %all-to-all-start.2) | async-done | bytes 131104 | tf_op jit(solution)/shard_map/all_to_all | solution.py:191
  88.8 0.1 shard_map.108
  88.9 0.7 copy.11
  (6 shorter events, 0.0 us)
Async XLA Ops:
  0.6 0.8 copy-start
  1.5 0.9 %copy-start.2 = (f32[128,256]{1,0:T(8,128)S(1)}, f32[128,256]{1,0:T(8,128)}, u32[]{:S(2)}) copy-start(f32[128,256]{1,0:T(8,128)} %taps_ref.1) | copy-start | bytes 393220
  2.4 0.8 copy-start.3
  3.2 44.1 %copy-start.7 = (f32[2,64,128]{2,1,0:T(8,128)S(1)}, f32[2,64,128]{2,1,0:T(8,128)}, u32[]{:S(2)}) copy-start(f32[2,64,128]{2,1,0:T(8,128)} %constant.12.clone.turn_ref) | copy-start | bytes 196612
  3.2 44.1 %copy-start.8 = (bf16[128,256]{1,0:T(8,128)(2,1)S(1)}, bf16[128,256]{1,0:T(8,128)(2,1)}, u32[]{:S(2)}) copy-start(bf16[128,256]{1,0:T(8,128)(2,1)} %constant.10.clone.first_ref) | copy-start | bytes 196612
  3.2 44.1 %copy-start.9 = (bf16[64,384]{1,0:T(8,128)(2,1)S(1)}, bf16[64,384]{1,0:T(8,128)(2,1)}, u32[]{:S(2)}) copy-start(bf16[64,384]{1,0:T(8,128)(2,1)} %constant.11.clone.last_ref) | copy-start | bytes 147460
  3.4 44.0 %copy-start.5 = (bf16[768,256]{1,0:T(8,128)(2,1)S(1)}, bf16[768,256]{1,0:T(8,128)(2,1)}, u32[]{:S(2)}) copy-start(bf16[768,256]{1,0:T(8,128)(2,1)} %constant.14.clone.inverse_ref) | copy-start | bytes 1179652
  3.4 44.0 %copy-start.6 = (bf16[768,256]{1,0:T(8,128)(2,1)S(1)}, bf16[768,256]{1,0:T(8,128)(2,1)}, u32[]{:S(2)}) copy-start(bf16[768,256]{1,0:T(8,128)(2,1)} %constant.13.clone.forward_ref) | copy-start | bytes 1179652
  75.6 7.9 %copy-start.1 = (bf16[1,128,256]{2,1,0:T(8,128)(2,1)S(1)}, bf16[1,128,256]{2,1,0:T(8,128)(2,1)}, u32[]{:S(2)}) copy-start(bf16[1,128,256]{2,1,0:T(8,128)(2,1)} %param.9) | copy-start | bytes 196612
  75.6 13.2 %all-to-all-start.2 = ((f32[8,32,128]{2,1,0:T(8,128)}), f32[8,32,128]{2,1,0:T(8,128)S(1)}, u32[]{:S(2)}, u32[]{:S(2)}) async-start(f32[8,32,128]{2,1,0:T(8,128)} %bitcast.8), calls=%async_computation.2 | async-start | bytes 262144 | tf_op jit(solution)/shard_map/all_to_all | solution.py:191
  83.5 0.7 copy-start.4

commit v2 on v1

v2 whole, which is shorter than its diff:
```python
import functools
import math

import jax
import jax.numpy as jnp
import ml_dtypes
import numpy as np
from jax import lax
from jax.experimental import pallas as pl
from jax.experimental.pallas import tpu as pltpu
from jax.sharding import PartitionSpec as P

SIDE = 128
HALF = 64
TOTAL = SIDE * SIDE
GROUP = 4
BLOCK = 32
SENT = 2 * GROUP + 1
BACK = GROUP + 1
MID = HALF + BLOCK
BF = jnp.bfloat16
F32 = jnp.float32


def halves(table):
    high = table.astype(ml_dtypes.bfloat16)
    low = (table - high.astype(np.float64)).astype(ml_dtypes.bfloat16)
    return high, low


def tables():
    blocks = np.arange(HALF)
    places = np.arange(SIDE)
    outer = 2.0 * math.pi * np.outer(np.arange(HALF) + 0.5, blocks) / SIDE
    first = np.concatenate([np.cos(outer), -np.sin(outer)], axis=0)
    high, low = halves(first)
    first_in = np.concatenate([high, low, high, low], axis=1)
    last = first.T * (2.0 / TOTAL)
    high, low = halves(last)
    last_out = np.concatenate([high, high, low], axis=1)
    angle = 2.0 * math.pi * np.outer(np.arange(HALF) + 0.5, places) / TOTAL
    turn = np.stack([np.cos(angle), -np.sin(angle)]).astype(np.float32)
    inner = 2.0 * math.pi * (np.outer(places, places) % SIDE) / SIDE
    cosine, sine = np.cos(inner), np.sin(inner)
    forward = np.block([[cosine, -sine], [sine, cosine]])
    inverse = np.block([[cosine, sine], [-sine, cosine]])
    high, low = halves(forward)
    forward = np.concatenate([high, high, low], axis=0)
    high, low = halves(inverse)
    inverse = np.concatenate([high, high, low], axis=0)
    return first_in, last_out, turn, forward, inverse


def split(value):
    high = value.astype(BF)
    return high, (value - high.astype(F32)).astype(BF)


def dot(left, right):
    return jnp.dot(left, right, preferred_element_type=F32)


def pack_kernel(own_ref, signal_hbm, grads_hbm, taps_hbm, out_ref, signal_ref, grads_ref, taps_ref, turned, sems):
    pairs = ((signal_hbm, signal_ref), (grads_hbm, grads_ref), (taps_hbm, taps_ref))
    copies = [pltpu.make_async_copy(src, dst, sems.at[i]) for i, (src, dst) in enumerate(pairs)]
    for copy in copies:
        copy.start()
    for kind, ref in enumerate((signal_ref, grads_ref)):
        copies[kind].wait()
        value = ref[...].astype(F32).T
        for block in range(2 * GROUP):
            odd, sub = divmod(block, GROUP)
            rows = value[BLOCK * block : BLOCK * (block + 1)]
            out_ref[pl.ds(SENT * odd + GROUP * kind + sub, BLOCK, stride=2 * SENT), :] = rows
    copies[2].wait()
    turned[...] = taps_ref[...].T
    sub = own_ref[0] // 2
    for odd in range(2):
        start = pl.multiple_of(BLOCK * (GROUP * odd + sub), BLOCK)
        out_ref[pl.ds(SENT * odd + 2 * GROUP, BLOCK, stride=2 * SENT), :] = turned[pl.ds(start, BLOCK), :]


def place(spread, turn_ref, index, column):
    cosine, sine = turn_ref[0], turn_ref[1]
    real, imag = column[:HALF], column[HALF:]
    real, imag = real * cosine - imag * sine, real * sine + imag * cosine
    keep(spread, index, real, imag)


def keep(ref, index, real, imag):
    rows = pl.ds(HALF * index, HALF)
    for part, value in enumerate((real, imag)):
        high, low = split(value)
        ref[rows, pl.ds(SIDE * part, SIDE)] = high
        ref[rows, pl.ds(2 * SIDE + SIDE * part, SIDE)] = low


def wide_dot(ref, table_ref):
    return dot(ref[...], table_ref[: 4 * SIDE]) + dot(ref[:, : 2 * SIDE], table_ref[4 * SIDE :])


def settle(back, last_ref, turn_ref):
    cosine, sine = turn_ref[0], turn_ref[1]
    results = []
    for index in range(0, GROUP, 2):
        stacks = []
        for one in (index, index + 1):
            rows = pl.ds(HALF * one, HALF)
            real, imag = back[rows, :SIDE], back[rows, SIDE:]
            value = jnp.concatenate(
                [real * cosine + imag * sine, imag * cosine - real * sine], axis=0
            )
            high, low = split(value)
            stacks.append(jnp.concatenate([high, low, high], axis=0))
        both = dot(last_ref[...], jnp.concatenate(stacks, axis=1))
        results += [both[:, :SIDE], both[:, SIDE:]]
    return results


def grad_kernel(own_ref, in_ref, first_ref, last_ref, turn_ref, forward_ref, inverse_ref, spec_ref, out_ref, spread, spectrum, mixed, back, taps):
    def load(row):
        return in_ref[pl.ds(row, HALF, stride=SENT), :]

    taps[...] = load(2 * GROUP)
    for sub in range(GROUP):
        pair = jnp.concatenate([load(sub), load(GROUP + sub)], axis=1).astype(BF)
        both = dot(first_ref[:, :SIDE], jnp.concatenate([pair, pair], axis=0))
        place(spread, turn_ref, sub, both[:, :SIDE])
        place(spread, turn_ref, GROUP + sub, both[:, SIDE:])
    spectrum[...] = wide_dot(spread, forward_ref)
    spec_ref[...] = spectrum[: GROUP * HALF]
    for sub in range(GROUP):
        parts = []
        for kind in range(2):
            rows = pl.ds(HALF * (GROUP * kind + sub), HALF)
            parts.append((spectrum[rows, :SIDE], spectrum[rows, SIDE:]))
        (sig_r, sig_i), (grad_r, grad_i) = parts
        keep(mixed, sub, grad_r * sig_r + grad_i * sig_i, grad_i * sig_r - grad_r * sig_i)
    back[...] = wide_dot(mixed, inverse_ref)
    for sub, value in enumerate(settle(back, last_ref, turn_ref)):
        for target in range(sub, 2 * GROUP, GROUP):
            out_ref[pl.ds(MID * target, HALF), :] = value
    start = pl.multiple_of(BLOCK * (own_ref[0] % 2), BLOCK)
    half = taps[pl.ds(start, BLOCK), :]
    for target in range(2 * GROUP):
        out_ref[pl.ds(MID * target + HALF, BLOCK), :] = half


def conv_kernel(in_ref, spec_ref, first_ref, last_ref, turn_ref, forward_ref, inverse_ref, out_ref, spread, spectrum, mixed, back):
    def taps(sub):
        starts = [MID * (2 * sub + core) + HALF for core in range(2)]
        return jnp.concatenate([in_ref[pl.ds(start, BLOCK), :] for start in starts], axis=0)

    for sub in range(0, GROUP, 2):
        high, low = split(jnp.concatenate([taps(sub), taps(sub + 1)], axis=1))
        both = dot(first_ref[...], jnp.concatenate([high, high, low, low], axis=0))
        place(spread, turn_ref, sub, both[:, :SIDE])
        place(spread, turn_ref, sub + 1, both[:, SIDE:])
    spectrum[...] = wide_dot(spread, forward_ref)
    for sub in range(GROUP):
        rows = pl.ds(HALF * sub, HALF)
        sig_r, sig_i = spec_ref[rows, :SIDE], spec_ref[rows, SIDE:]
        filt_r, filt_i = spectrum[rows, :SIDE], spectrum[rows, SIDE:]
        keep(mixed, sub, sig_r * filt_r - sig_i * filt_i, sig_r * filt_i + sig_i * filt_r)
    back[...] = wide_dot(mixed, inverse_ref)
    for sub, value in enumerate(settle(back, last_ref, turn_ref)):
        out_ref[pl.ds(sub, HALF, stride=BACK), :] = value
    total = in_ref[pl.ds(0, HALF), :]
    for source in range(1, 2 * GROUP):
        total = total + in_ref[pl.ds(MID * source, HALF), :]
    out_ref[pl.ds(GROUP, HALF, stride=BACK), :] = total


def finish_kernel(own_ref, in_ref, signal_ref, gain_ref, out_ref, grad_ref):
    def load(odd, row):
        return in_ref[pl.ds(BACK * odd + row, BLOCK, stride=2 * BACK), :]

    conv = jnp.concatenate([load(*divmod(block, GROUP)) for block in range(2 * GROUP)], axis=0)
    out_ref[...] = (conv.T + gain_ref[...] * signal_ref[...].astype(F32)).astype(BF)
    odd = own_ref[0] // GROUP
    grad_ref[...] = jnp.where(odd == 0, load(0, GROUP), load(1, GROUP))


def call(kernel, shapes, *args, flops=1000, scratch=(), hbm=False, scalar=False):
    outs = [jax.ShapeDtypeStruct(*one) for one in shapes]
    size = sum(math.prod(a.shape) * a.dtype.itemsize for a in [*args, *outs])
    vmem = pl.BlockSpec(memory_space=pltpu.VMEM)
    place_in = pl.BlockSpec(memory_space=pltpu.HBM) if hbm else vmem
    specs = [place_in] * len(args)
    if scalar:
        specs[0] = pl.BlockSpec(memory_space=pltpu.SMEM)
    result = pl.pallas_call(
        kernel,
        out_shape=outs,
        in_specs=specs,
        out_specs=[vmem] * len(outs),
        scratch_shapes=list(scratch),
        cost_estimate=pl.CostEstimate(flops=flops, bytes_accessed=size, transcendentals=0),
        compiler_params=pltpu.CompilerParams(vmem_limit_bytes=58000000 if hbm else 24 * 1024 * 1024),
    )(*args)
    return result if len(shapes) > 1 else result[0]


def exchange(rows, axis, inner):
    parts = lax.axis_size(axis)
    blocks = rows.reshape((parts, *inner, rows.shape[-1]))
    return lax.all_to_all(blocks, axis, split_axis=0, concat_axis=0, tiled=True).reshape(rows.shape)


def body(inputs, cotangent, filter_taps, skip_gain):
    _, rows, chans = inputs.shape
    parts, shares = lax.axis_size("seq"), lax.axis_size("dp")
    own = lax.axis_index("dp").astype(jnp.int32)[None]
    signal = inputs[0]
    wide = 2 * SIDE
    constants = [jnp.asarray(t) for t in tables()]

    def room(count):
        return (
            pltpu.VMEM((count * GROUP * HALF, 2 * wide), BF),
            pltpu.VMEM((count * GROUP * HALF, wide), F32),
            pltpu.VMEM((GROUP * HALF, 2 * wide), BF),
            pltpu.VMEM((GROUP * HALF, wide), F32),
        )

    packed = call(
        pack_kernel,
        [((SENT * parts, rows), F32)],
        own,
        signal,
        cotangent[0],
        filter_taps,
        hbm=True,
        scalar=True,
        scratch=(
            pltpu.VMEM((rows, chans), BF),
            pltpu.VMEM((rows, chans), BF),
            pltpu.VMEM((rows, chans), F32),
            pltpu.VMEM((chans, rows), F32),
            pltpu.SemaphoreType.DMA((3,)),
        ),
    )
    columns = exchange(packed, "seq", (SENT, 1))
    spec, partial = call(
        grad_kernel,
        [((GROUP * HALF, wide), F32), ((MID * shares, rows), F32)],
        own,
        columns,
        *constants,
        flops=500_000_000,
        scalar=True,
        scratch=(*room(2), pltpu.VMEM((HALF, rows), F32)),
    )
    partial = exchange(partial, "dp", (MID,))
    settled = call(
        conv_kernel,
        [((BACK * parts, rows), F32)],
        partial,
        spec,
        *constants,
        flops=500_000_000,
        scratch=room(1),
    )
    settled = exchange(settled, "seq", (BACK, 1))
    outputs, filter_grad = call(
        finish_kernel,
        [((rows, chans), BF), ((chans // shares, rows), F32)],
        own,
        settled,
        signal,
        skip_gain[None],
        scalar=True,
    )
    return outputs[None], filter_grad.T


def solution(mesh):
    placed = (P("dp", "seq", None), P("dp", "seq", None), P("seq", None), P())
    return jax.shard_map(
        body,
        mesh=mesh,
        in_specs=placed,
        out_specs=(P("dp", "seq", None), P("seq", "dp")),
        check_vma=False,
    )
```

time: 90 us -> 83.8 us (0.931); the launches traced: 89.6 us -> 82.3 us
  starting transfers between devices: 7.88 us -> 0 us
  blocking collectives: 69.8 us -> 76 us
  waiting for transfers between devices: 3.86 us -> 0 us
  local copies, waits for them, and re-layouts: 3.96 us -> 0.72 us
  Pallas kernels: 3.34 us -> 4.88 us
    all_to_all x1 -> x0, starting transfers between devices: 7.88 us -> none  [body(): lax.all_to_all(partial, 'dp', split_axis=0, concat_axis=0, tiled=True)]
    all_to_all x2 -> x3, blocking collectives: 69.8 us -> 76 us  [exchange(): lax.all_to_all(blocks, axis, split_axis=0, concat_axis=0, tiled=True)]
    all_to_all x1 -> x0, waiting for transfers between devices: 3.86 us -> none  [body(): lax.all_to_all(partial, 'dp', split_axis=0, concat_axis=0, tiled=True)]
    unnamed x21 -> x14, local copies, waits for them, and re-layouts: 3.96 us -> 0.72 us
    pallas_call x5 -> x4, Pallas kernels: 3.34 us -> 4.88 us  [call(): pl.pallas_call(kernel, out_shape=outs, in_specs=specs, out_specs=[vmem] *...]
  transfers between devices with their start and end apart: 1 -> 0, of which waited for: 1 -> 0; matrix products, arithmetic and copies ran while one was open for 0% -> 0% of each run, Pallas kernels for 1% -> 0%
where the time goes in v2:
time: 83.8 us; the launch traced here: 82.3 us
  blocking collectives  76 us (91%)
  Pallas kernels  4.88 us (6%)
    all_to_all x3, blocking collectives, exchange(): lax.all_to_all(blocks, axis, split_axis=0, concat_axis=0, tiled=True)  76 us
    pallas_call x4, Pallas kernels, call(): pl.pallas_call(kernel, out_shape=outs, in_specs=specs, out_specs=[vmem] *...  4.88 us

profile of v2, /device:TPU:1, one launch (start us, length us, event | category | flops | bytes accessed | tf_op | source)
XLA Modules:
  0.0 82.3 jit_solution(17901049622137368185)
XLA Ops:
  0.6 0.0 copy-start.3
  0.6 1.9 %shard_map.104 = f32[576,128]{1,0:T(8,128)} custom-call(s32[1]{0:T(128)} %bitcast.own_ref, bf16[128,256]{1,0:T(8,128)(2,1)} %bitcast.16, bf16[128,256]{1,0:T(8,128)(2,1)} %bitcast.21, f32[128,256]{1,0:T(8,128)} %taps_hbm.1), custom_call_target="tpu_custom_call" | custom-call | flops 1000 | bytes 557060 | tf_op jit(solution)/shard_map/pallas_call | solution.py:192
  2.6 0.0 copy-start.2
  2.6 0.0 copy-start.4
  2.6 0.0 copy-start.5
  2.6 0.0 copy-start.6
  2.7 39.4 %all_to_all.15 = f32[64,9,1,128]{3,2,1,0:T(1,128)S(1)} all-to-all(f32[64,9,1,128]{3,2,1,0:T(1,128)} %bitcast.20), channel_id=1, replica_groups=mesh['seq'=64,'dp'=8] {'seq'}, dimensions={0} | all-to-all | bytes 589824 | tf_op jit(solution)/shard_map/all_to_all | solution.py:207
  42.1 0.0 copy-done.3
  42.1 0.0 copy-done.2
  42.1 0.0 copy-done.4
  42.1 0.0 copy-done.5
  42.1 0.0 copy-done.6
  42.1 1.2 %shard_map.105 = (f32[256,256]{1,0:T(8,128)S(1)}, f32[768,128]{1,0:T(8,128)S(1)}) custom-call(s32[1]{0:T(128)} %bitcast.own_ref, f32[576,128]{1,0:T(8,128)S(1)} %bitcast.15, bf16[128,256]{1,0:T(8,128)(2,1)S(1)} %copy-done.5, bf16[64,384]{1,0:T(8,128)(2,1)S(1)} %copy-done.6, f32[2,64,128]{2,1,0:T(8,128)S(1)} %copy-done.4, bf16[768,256]{1,0:T(8,128)(2,1)S(1)} %copy-done.3, ...), custom_call_target="tpu_custom_call" | custom-call | flops 500000000 | bytes 1916932 | tf_op jit(solution)/shard_map/pallas_call | solution.py:192
  43.4 15.4 %all_to_all.16 = f32[8,96,128]{2,1,0:T(8,128)S(1)} all-to-all(f32[8,96,128]{2,1,0:T(8,128)S(1)} %bitcast.14), channel_id=1, replica_groups=mesh['seq'=64,'dp'=8] {'dp'}, dimensions={0} | all-to-all | bytes 786432 | tf_op jit(solution)/shard_map/all_to_all | solution.py:207
  58.8 1.0 %shard_map.106 = f32[320,128]{1,0:T(8,128)S(1)} custom-call(f32[768,128]{1,0:T(8,128)S(1)} %bitcast.13, f32[256,256]{1,0:T(8,128)S(1)} %get-tuple-element.7.spec_ref, bf16[128,256]{1,0:T(8,128)(2,1)S(1)} %copy-done.5, bf16[64,384]{1,0:T(8,128)(2,1)S(1)} %copy-done.6, f32[2,64,128]{2,1,0:T(8,128)S(1)} %copy-done.4, bf16[768,256]{1,0:T(8,128)(2,1)S(1)} %copy-done.3, ...), custom_call_target="tpu_custom_call" | custom-call | flops 500000000 | bytes 1785856 | tf_op jit(solution)/shard_map/pallas_call | solution.py:192
  59.8 0.0 copy-start
  59.8 21.1 %all_to_all.17 = f32[64,5,1,128]{3,2,1,0:T(1,128)S(1)} all-to-all(f32[64,5,1,128]{3,2,1,0:T(1,128)S(1)} %bitcast.18), channel_id=1, replica_groups=mesh['seq'=64,'dp'=8] {'seq'}, dimensions={0} | all-to-all | bytes 327680 | tf_op jit(solution)/shard_map/all_to_all | solution.py:207
  80.9 0.0 copy-start.1
  80.9 0.0 copy-done
  80.9 0.7 copy-done.1
  81.6 0.7 shard_map.107
Async XLA Ops:
  0.6 41.5 %copy-start.3 = (bf16[768,256]{1,0:T(8,128)(2,1)S(1)}, bf16[768,256]{1,0:T(8,128)(2,1)}, u32[]{:S(2)}) copy-start(bf16[768,256]{1,0:T(8,128)(2,1)} %constant.17.clone.forward_ref) | copy-start | bytes 1179652
  2.6 39.5 %copy-start.2 = (bf16[768,256]{1,0:T(8,128)(2,1)S(1)}, bf16[768,256]{1,0:T(8,128)(2,1)}, u32[]{:S(2)}) copy-start(bf16[768,256]{1,0:T(8,128)(2,1)} %constant.18.clone.inverse_ref) | copy-start | bytes 1179652
  2.6 39.5 %copy-start.4 = (f32[2,64,128]{2,1,0:T(8,128)S(1)}, f32[2,64,128]{2,1,0:T(8,128)}, u32[]{:S(2)}) copy-start(f32[2,64,128]{2,1,0:T(8,128)} %constant.16.clone.turn_ref) | copy-start | bytes 196612
  2.6 39.5 %copy-start.5 = (bf16[128,256]{1,0:T(8,128)(2,1)S(1)}, bf16[128,256]{1,0:T(8,128)(2,1)}, u32[]{:S(2)}) copy-start(bf16[128,256]{1,0:T(8,128)(2,1)} %constant.14.clone.first_ref) | copy-start | bytes 196612
  2.6 39.5 %copy-start.6 = (bf16[64,384]{1,0:T(8,128)(2,1)S(1)}, bf16[64,384]{1,0:T(8,128)(2,1)}, u32[]{:S(2)}) copy-start(bf16[64,384]{1,0:T(8,128)(2,1)} %constant.15.clone.last_ref) | copy-start | bytes 147460
  59.8 21.1 %copy-start = (bf16[1,128,256]{2,1,0:T(8,128)(2,1)S(1)}, bf16[1,128,256]{2,1,0:T(8,128)(2,1)}, u32[]{:S(2)}) copy-start(bf16[1,128,256]{2,1,0:T(8,128)(2,1)} %param.9) | copy-start | bytes 196612
  80.9 0.7 copy-start.1

commit v3 on v2

--- a/solution.py
+++ b/solution.py
@@ -60,8 +60,8 @@
     return jnp.dot(left, right, preferred_element_type=F32)
 
 
-def pack_kernel(own_ref, signal_hbm, grads_hbm, taps_hbm, out_ref, signal_ref, grads_ref, taps_ref, turned, sems):
-    pairs = ((signal_hbm, signal_ref), (grads_hbm, grads_ref), (taps_hbm, taps_ref))
+def pack_kernel(own_ref, seat_ref, signal_hbm, grads_hbm, taps_hbm, gain_hbm, out_ref, signal_ref, grads_ref, taps_ref, gain_ref, turned, sems):
+    pairs = ((signal_hbm, signal_ref), (grads_hbm, grads_ref), (taps_hbm, taps_ref), (gain_hbm, gain_ref))
     copies = [pltpu.make_async_copy(src, dst, sems.at[i]) for i, (src, dst) in enumerate(pairs)]
     for copy in copies:
         copy.start()
@@ -73,6 +73,12 @@
             rows = value[BLOCK * block : BLOCK * (block + 1)]
             out_ref[pl.ds(SENT * odd + GROUP * kind + sub, BLOCK, stride=2 * SENT), :] = rows
     copies[2].wait()
+    copies[3].wait()
+
+    @pl.when(seat_ref[0] == 0)
+    def _():
+        taps_ref[:1] = taps_ref[:1] + gain_ref[...]
+
     turned[...] = taps_ref[...].T
     sub = own_ref[0] // 2
     for odd in range(2):
@@ -171,24 +177,23 @@
     out_ref[pl.ds(GROUP, HALF, stride=BACK), :] = total
 
 
-def finish_kernel(own_ref, in_ref, signal_ref, gain_ref, out_ref, grad_ref):
+def finish_kernel(own_ref, in_ref, out_ref, grad_ref):
     def load(odd, row):
         return in_ref[pl.ds(BACK * odd + row, BLOCK, stride=2 * BACK), :]
 
     conv = jnp.concatenate([load(*divmod(block, GROUP)) for block in range(2 * GROUP)], axis=0)
-    out_ref[...] = (conv.T + gain_ref[...] * signal_ref[...].astype(F32)).astype(BF)
+    out_ref[...] = conv.T.astype(BF)
     odd = own_ref[0] // GROUP
     grad_ref[...] = jnp.where(odd == 0, load(0, GROUP), load(1, GROUP))
 
 
-def call(kernel, shapes, *args, flops=1000, scratch=(), hbm=False, scalar=False):
+def call(kernel, shapes, *args, flops=1000, scratch=(), hbm=False, scalars=0):
     outs = [jax.ShapeDtypeStruct(*one) for one in shapes]
     size = sum(math.prod(a.shape) * a.dtype.itemsize for a in [*args, *outs])
     vmem = pl.BlockSpec(memory_space=pltpu.VMEM)
     place_in = pl.BlockSpec(memory_space=pltpu.HBM) if hbm else vmem
     specs = [place_in] * len(args)
-    if scalar:
-        specs[0] = pl.BlockSpec(memory_space=pltpu.SMEM)
+    specs[:scalars] = [pl.BlockSpec(memory_space=pltpu.SMEM)] * scalars
     result = pl.pallas_call(
         kernel,
         out_shape=outs,
@@ -211,7 +216,7 @@
     _, rows, chans = inputs.shape
     parts, shares = lax.axis_size("seq"), lax.axis_size("dp")
     own = lax.axis_index("dp").astype(jnp.int32)[None]
-    signal = inputs[0]
+    seat = lax.axis_index("seq").astype(jnp.int32)[None]
     wide = 2 * SIDE
     constants = [jnp.asarray(t) for t in tables()]
 
@@ -227,17 +232,20 @@
         pack_kernel,
         [((SENT * parts, rows), F32)],
         own,
-        signal,
+        seat,
+        inputs[0],
         cotangent[0],
         filter_taps,
+        skip_gain[None],
         hbm=True,
-        scalar=True,
+        scalars=2,
         scratch=(
             pltpu.VMEM((rows, chans), BF),
             pltpu.VMEM((rows, chans), BF),
             pltpu.VMEM((rows, chans), F32),
+            pltpu.VMEM((1, chans), F32),
             pltpu.VMEM((chans, rows), F32),
-            pltpu.SemaphoreType.DMA((3,)),
+            pltpu.SemaphoreType.DMA((4,)),
         ),
     )
     columns = exchange(packed, "seq", (SENT, 1))
@@ -248,7 +256,7 @@
         columns,
         *constants,
         flops=500_000_000,
-        scalar=True,
+        scalars=1,
         scratch=(*room(2), pltpu.VMEM((HALF, rows), F32)),
     )
     partial = exchange(partial, "dp", (MID,))
@@ -267,9 +275,7 @@
         [((rows, chans), BF), ((chans // shares, rows), F32)],
         own,
         settled,
-        signal,
-        skip_gain[None],
-        scalar=True,
+        scalars=1,
     )
     return outputs[None], filter_grad.T
 

time: 83.8 us -> 82.9 us (0.989)
  no operation moved by 1% of the time
where the time goes in v3:
time: 82.9 us; the launch traced here: 81.5 us
  blocking collectives  75.8 us (91%)
  Pallas kernels  4.89 us (6%)
    all_to_all x3, blocking collectives, exchange(): lax.all_to_all(blocks, axis, split_axis=0, concat_axis=0, tiled=True)  75.8 us
    pallas_call x4, Pallas kernels, call(): pl.pallas_call(kernel, out_shape=outs, in_specs=specs, out_specs=[vmem] *...  4.89 us

profile of v3, /device:TPU:1, one launch (start us, length us, event | category | flops | bytes accessed | tf_op | source)
XLA Modules:
  0.0 81.5 jit_solution(17983302411318323408)
XLA Ops:
  0.6 0.0 copy-start.1
  0.6 1.9 %shard_map.104 = f32[576,128]{1,0:T(8,128)} custom-call(s32[1]{0:T(128)} %bitcast.own_ref, s32[1]{0:T(128)} %bitcast.1.seat_ref, bf16[128,256]{1,0:T(8,128)(2,1)} %bitcast.19, bf16[128,256]{1,0:T(8,128)(2,1)} %bitcast.20, f32[128,256]{1,0:T(8,128)} %taps_hbm.1, f32[1,256]{1,0:T(1,128)} %bitcast.21), custom_call_target="tpu_custom_call" | custom-call | flops 1000 | bytes 558088 | tf_op jit(solution)/shard_map/pallas_call | solution.py:197
  2.6 0.0 copy-start
  2.6 0.0 copy-start.2
  2.6 0.0 copy-start.3
  2.6 0.0 copy-start.4
  2.7 39.4 %all_to_all.15 = f32[64,9,1,128]{3,2,1,0:T(1,128)S(1)} all-to-all(f32[64,9,1,128]{3,2,1,0:T(1,128)} %bitcast.18), channel_id=1, replica_groups=mesh['seq'=64,'dp'=8] {'seq'}, dimensions={0} | all-to-all | bytes 589824 | tf_op jit(solution)/shard_map/all_to_all | solution.py:212
  42.1 0.0 copy-done.1
  42.1 0.0 copy-done
  42.1 0.0 copy-done.2
  42.1 0.0 copy-done.3
  42.1 0.0 copy-done.4
  42.1 1.2 %shard_map.105 = (f32[256,256]{1,0:T(8,128)S(1)}, f32[768,128]{1,0:T(8,128)S(1)}) custom-call(s32[1]{0:T(128)} %bitcast.own_ref, f32[576,128]{1,0:T(8,128)S(1)} %bitcast.16, bf16[128,256]{1,0:T(8,128)(2,1)S(1)} %copy-done.3, bf16[64,384]{1,0:T(8,128)(2,1)S(1)} %copy-done.4, f32[2,64,128]{2,1,0:T(8,128)S(1)} %copy-done.2, bf16[768,256]{1,0:T(8,128)(2,1)S(1)} %copy-done.1, ...), custom_call_target="tpu_custom_call" | custom-call | flops 500000000 | bytes 1916932 | tf_op jit(solution)/shard_map/pallas_call | solution.py:197
  43.4 15.4 %all_to_all.16 = f32[8,96,128]{2,1,0:T(8,128)S(1)} all-to-all(f32[8,96,128]{2,1,0:T(8,128)S(1)} %bitcast.15), channel_id=1, replica_groups=mesh['seq'=64,'dp'=8] {'dp'}, dimensions={0} | all-to-all | bytes 786432 | tf_op jit(solution)/shard_map/all_to_all | solution.py:212
  58.8 1.0 %shard_map.106 = f32[320,128]{1,0:T(8,128)S(1)} custom-call(f32[768,128]{1,0:T(8,128)S(1)} %bitcast.14, f32[256,256]{1,0:T(8,128)S(1)} %get-tuple-element.7.spec_ref, bf16[128,256]{1,0:T(8,128)(2,1)S(1)} %copy-done.3, bf16[64,384]{1,0:T(8,128)(2,1)S(1)} %copy-done.4, f32[2,64,128]{2,1,0:T(8,128)S(1)} %copy-done.2, bf16[768,256]{1,0:T(8,128)(2,1)S(1)} %copy-done.1, ...), custom_call_target="tpu_custom_call" | custom-call | flops 500000000 | bytes 1785856 | tf_op jit(solution)/shard_map/pallas_call | solution.py:197
  59.8 20.9 %all_to_all.17 = f32[64,5,1,128]{3,2,1,0:T(1,128)S(1)} all-to-all(f32[64,5,1,128]{3,2,1,0:T(1,128)S(1)} %bitcast.17), channel_id=1, replica_groups=mesh['seq'=64,'dp'=8] {'seq'}, dimensions={0} | all-to-all | bytes 327680 | tf_op jit(solution)/shard_map/all_to_all | solution.py:212
  80.7 0.7 shard_map.107
Async XLA Ops:
  0.6 41.5 %copy-start.1 = (bf16[768,256]{1,0:T(8,128)(2,1)S(1)}, bf16[768,256]{1,0:T(8,128)(2,1)}, u32[]{:S(2)}) copy-start(bf16[768,256]{1,0:T(8,128)(2,1)} %constant.22.clone.forward_ref) | copy-start | bytes 1179652
  2.6 39.5 %copy-start = (bf16[768,256]{1,0:T(8,128)(2,1)S(1)}, bf16[768,256]{1,0:T(8,128)(2,1)}, u32[]{:S(2)}) copy-start(bf16[768,256]{1,0:T(8,128)(2,1)} %constant.23.clone.inverse_ref) | copy-start | bytes 1179652
  2.6 39.5 %copy-start.2 = (f32[2,64,128]{2,1,0:T(8,128)S(1)}, f32[2,64,128]{2,1,0:T(8,128)}, u32[]{:S(2)}) copy-start(f32[2,64,128]{2,1,0:T(8,128)} %constant.21.clone.turn_ref) | copy-start | bytes 196612
  2.6 39.5 %copy-start.3 = (bf16[128,256]{1,0:T(8,128)(2,1)S(1)}, bf16[128,256]{1,0:T(8,128)(2,1)}, u32[]{:S(2)}) copy-start(bf16[128,256]{1,0:T(8,128)(2,1)} %constant.19.clone.first_ref) | copy-start | bytes 196612
  2.6 39.5 %copy-start.4 = (bf16[64,384]{1,0:T(8,128)(2,1)S(1)}, bf16[64,384]{1,0:T(8,128)(2,1)}, u32[]{:S(2)}) copy-start(bf16[64,384]{1,0:T(8,128)(2,1)} %constant.20.clone.last_ref) | copy-start | bytes 147460

commit v4 on v3

--- a/solution.py
+++ b/solution.py
@@ -17,7 +17,7 @@
 BLOCK = 32
 SENT = 2 * GROUP + 1
 BACK = GROUP + 1
-MID = HALF + BLOCK
+MID = 2 * HALF
 BF = jnp.bfloat16
 F32 = jnp.float32
 
@@ -68,10 +68,9 @@
     for kind, ref in enumerate((signal_ref, grads_ref)):
         copies[kind].wait()
         value = ref[...].astype(F32).T
-        for block in range(2 * GROUP):
-            odd, sub = divmod(block, GROUP)
-            rows = value[BLOCK * block : BLOCK * (block + 1)]
-            out_ref[pl.ds(SENT * odd + GROUP * kind + sub, BLOCK, stride=2 * SENT), :] = rows
+        for sub in range(GROUP):
+            rows = value[HALF * sub : HALF * (sub + 1)]
+            out_ref[pl.ds(GROUP * kind + sub, HALF, stride=SENT), :] = rows
     copies[2].wait()
     copies[3].wait()
 
@@ -80,10 +79,8 @@
         taps_ref[:1] = taps_ref[:1] + gain_ref[...]
 
     turned[...] = taps_ref[...].T
-    sub = own_ref[0] // 2
-    for odd in range(2):
-        start = pl.multiple_of(BLOCK * (GROUP * odd + sub), BLOCK)
-        out_ref[pl.ds(SENT * odd + 2 * GROUP, BLOCK, stride=2 * SENT), :] = turned[pl.ds(start, BLOCK), :]
+    start = pl.multiple_of(HALF * (own_ref[0] // 2), HALF)
+    out_ref[pl.ds(2 * GROUP, HALF, stride=SENT), :] = turned[pl.ds(start, HALF), :]
 
 
 def place(spread, turn_ref, index, column):
@@ -123,11 +120,13 @@
     return results
 
 
-def grad_kernel(own_ref, in_ref, first_ref, last_ref, turn_ref, forward_ref, inverse_ref, spec_ref, out_ref, spread, spectrum, mixed, back, taps):
+def grad_kernel(in_ref, first_ref, last_ref, turn_ref, forward_ref, inverse_ref, spec_ref, out_ref, spread, spectrum, mixed, back):
     def load(row):
         return in_ref[pl.ds(row, HALF, stride=SENT), :]
 
-    taps[...] = load(2 * GROUP)
+    taps = load(2 * GROUP)
+    for target in range(GROUP):
+        out_ref[pl.ds(MID * target + HALF, HALF), :] = taps
     for sub in range(GROUP):
         pair = jnp.concatenate([load(sub), load(GROUP + sub)], axis=1).astype(BF)
         both = dot(first_ref[:, :SIDE], jnp.concatenate([pair, pair], axis=0))
@@ -144,18 +143,12 @@
         keep(mixed, sub, grad_r * sig_r + grad_i * sig_i, grad_i * sig_r - grad_r * sig_i)
     back[...] = wide_dot(mixed, inverse_ref)
     for sub, value in enumerate(settle(back, last_ref, turn_ref)):
-        for target in range(sub, 2 * GROUP, GROUP):
-            out_ref[pl.ds(MID * target, HALF), :] = value
-    start = pl.multiple_of(BLOCK * (own_ref[0] % 2), BLOCK)
-    half = taps[pl.ds(start, BLOCK), :]
-    for target in range(2 * GROUP):
-        out_ref[pl.ds(MID * target + HALF, BLOCK), :] = half
+        out_ref[pl.ds(MID * sub, HALF), :] = value
 
 
 def conv_kernel(in_ref, spec_ref, first_ref, last_ref, turn_ref, forward_ref, inverse_ref, out_ref, spread, spectrum, mixed, back):
     def taps(sub):
-        starts = [MID * (2 * sub + core) + HALF for core in range(2)]
-        return jnp.concatenate([in_ref[pl.ds(start, BLOCK), :] for start in starts], axis=0)
+        return in_ref[pl.ds(MID * sub + HALF, HALF), :]
 
     for sub in range(0, GROUP, 2):
         high, low = split(jnp.concatenate([taps(sub), taps(sub + 1)], axis=1))
@@ -172,19 +165,21 @@
     for sub, value in enumerate(settle(back, last_ref, turn_ref)):
         out_ref[pl.ds(sub, HALF, stride=BACK), :] = value
     total = in_ref[pl.ds(0, HALF), :]
-    for source in range(1, 2 * GROUP):
+    for source in range(1, GROUP):
         total = total + in_ref[pl.ds(MID * source, HALF), :]
     out_ref[pl.ds(GROUP, HALF, stride=BACK), :] = total
 
 
-def finish_kernel(own_ref, in_ref, out_ref, grad_ref):
-    def load(odd, row):
-        return in_ref[pl.ds(BACK * odd + row, BLOCK, stride=2 * BACK), :]
-
-    conv = jnp.concatenate([load(*divmod(block, GROUP)) for block in range(2 * GROUP)], axis=0)
-    out_ref[...] = conv.T.astype(BF)
-    odd = own_ref[0] // GROUP
-    grad_ref[...] = jnp.where(odd == 0, load(0, GROUP), load(1, GROUP))
+def part_kernel(own_ref, in_ref, send_ref, keep_ref):
+    low, high = [in_ref[pl.ds(BACK * BLOCK * half + GROUP, BLOCK, stride=BACK), :] for half in range(2)]
+    first = own_ref[0] % 2 == 0
+    send_ref[...] = jnp.where(first, high, low)
+    keep_ref[...] = jnp.where(first, low, high)
+
+
+def finish_kernel(in_ref, out_ref):
+    rows = [in_ref[pl.ds(sub, HALF, stride=BACK), :] for sub in range(GROUP)]
+    out_ref[...] = jnp.concatenate(rows, axis=0).T.astype(BF)
 
 
 def call(kernel, shapes, *args, flops=1000, scratch=(), hbm=False, scalars=0):
@@ -206,10 +201,10 @@
     return result if len(shapes) > 1 else result[0]
 
 
-def exchange(rows, axis, inner):
-    parts = lax.axis_size(axis)
+def exchange(rows, axis, inner, groups=None):
+    parts = len(groups[0]) if groups else lax.axis_size(axis)
     blocks = rows.reshape((parts, *inner, rows.shape[-1]))
-    return lax.all_to_all(blocks, axis, split_axis=0, concat_axis=0, tiled=True).reshape(rows.shape)
+    return lax.all_to_all(blocks, axis, split_axis=0, concat_axis=0, tiled=True, axis_index_groups=groups).reshape(rows.shape)
 
 
 def body(inputs, cotangent, filter_taps, skip_gain):
@@ -251,15 +246,14 @@
     columns = exchange(packed, "seq", (SENT, 1))
     spec, partial = call(
         grad_kernel,
-        [((GROUP * HALF, wide), F32), ((MID * shares, rows), F32)],
-        own,
+        [((GROUP * HALF, wide), F32), ((MID * GROUP, rows), F32)],
         columns,
         *constants,
         flops=500_000_000,
-        scalars=1,
-        scratch=(*room(2), pltpu.VMEM((HALF, rows), F32)),
-    )
-    partial = exchange(partial, "dp", (MID,))
+        scratch=room(2),
+    )
+    groups = [list(range(core, shares, 2)) for core in range(2)]
+    partial = exchange(partial, "dp", (MID,), groups)
     settled = call(
         conv_kernel,
         [((BACK * parts, rows), F32)],
@@ -270,13 +264,11 @@
         scratch=room(1),
     )
     settled = exchange(settled, "seq", (BACK, 1))
-    outputs, filter_grad = call(
-        finish_kernel,
-        [((rows, chans), BF), ((chans // shares, rows), F32)],
-        own,
-        settled,
-        scalars=1,
-    )
+    shape = ((chans // shares, rows), F32)
+    send, held = call(part_kernel, [shape, shape], own, settled, scalars=1)
+    got = lax.ppermute(send, "dp", [(one, one ^ 1) for one in range(shares)])
+    outputs = call(finish_kernel, [((rows, chans), BF)], settled, flops=500_000_000)
+    filter_grad = held + got
     return outputs[None], filter_grad.T
 
 

time: 82.9 us -> 83.7 us (level); the launches traced: 81.5 us -> 83.4 us
  starting transfers between devices: 0 us -> 6.25 us
  blocking collectives: 75.8 us -> 70.8 us
    ppermute x0 -> x1, starting transfers between devices: none -> 6.25 us  [body(): got = lax.ppermute(send, 'dp', [(one, one ^ 1) for one in range(shares)])]
    all_to_all x3, blocking collectives: 75.8 us -> 70.8 us  [exchange(): lax.all_to_all(blocks, axis, split_axis=0, concat_axis=0, tiled=True, axi...]
    pallas_call x4 -> x5, Pallas kernels: 4.89 us -> 4.89 us  [call(): pl.pallas_call(kernel, out_shape=outs, in_specs=specs, out_specs=[vmem] *...]
  transfers between devices with their start and end apart: 0 -> 1, of which waited for: 0 -> 1; matrix products, arithmetic and copies ran while one was open for 0% -> 0% of each run, Pallas kernels for 0% -> 1%
where the time goes in v4:
time: 83.7 us; the launch traced here: 83.4 us
  blocking collectives  70.8 us (85%)
  starting transfers between devices  6.25 us (7%)
  Pallas kernels  4.89 us (6%)
    all_to_all x3, blocking collectives, exchange(): lax.all_to_all(blocks, axis, split_axis=0, concat_axis=0, tiled=True, axi...  70.8 us
    ppermute x1, starting transfers between devices, body(): got = lax.ppermute(send, 'dp', [(one, one ^ 1) for one in range(shares)])  6.25 us
    pallas_call x5, Pallas kernels, call(): pl.pallas_call(kernel, out_shape=outs, in_specs=specs, out_specs=[vmem] *...  4.89 us
  transfers between devices with their start and end apart: 1, of which 1 were waited for; matrix products, arithmetic and copies ran while one was open for 0% of the time, Pallas kernels for 1%

profile of v4, /device:TPU:1, one launch (start us, length us, event | category | flops | bytes accessed | tf_op | source)
XLA Modules:
  0.0 83.4 jit_solution(18234121663612625335)
XLA Ops:
  0.6 0.0 copy-start.1
  0.6 2.0 %shard_map.104 = f32[576,128]{1,0:T(8,128)} custom-call(s32[1]{0:T(128)} %bitcast.own_ref, s32[1]{0:T(128)} %bitcast.1.seat_ref, bf16[128,256]{1,0:T(8,128)(2,1)} %bitcast.21, bf16[128,256]{1,0:T(8,128)(2,1)} %bitcast.22, f32[128,256]{1,0:T(8,128)} %taps_hbm.1, f32[1,256]{1,0:T(1,128)} %bitcast.23), custom_call_target="tpu_custom_call" | custom-call | flops 1000 | bytes 558088 | tf_op jit(solution)/shard_map/pallas_call | solution.py:192
  2.6 0.0 copy-start
  2.6 0.0 copy-start.2
  2.6 0.0 copy-start.3
  2.6 0.0 copy-start.4
  2.7 39.4 %all_to_all.15 = f32[64,9,1,128]{3,2,1,0:T(1,128)S(1)} all-to-all(f32[64,9,1,128]{3,2,1,0:T(1,128)} %bitcast.20), channel_id=1, replica_groups=mesh['seq'=64,'dp'=8] {'seq'}, dimensions={0} | all-to-all | bytes 589824 | tf_op jit(solution)/shard_map/all_to_all | solution.py:207
  42.1 0.0 copy-done.1
  42.1 0.0 copy-done
  42.1 0.0 copy-done.2
  42.1 0.0 copy-done.3
  42.1 0.0 copy-done.4
  42.1 1.2 %shard_map.105 = (f32[256,256]{1,0:T(8,128)S(1)}, f32[512,128]{1,0:T(8,128)S(1)}) custom-call(f32[576,128]{1,0:T(8,128)S(1)} %bitcast.16, bf16[128,256]{1,0:T(8,128)(2,1)S(1)} %copy-done.3, bf16[64,384]{1,0:T(8,128)(2,1)S(1)} %copy-done.4, f32[2,64,128]{2,1,0:T(8,128)S(1)} %copy-done.2, bf16[768,256]{1,0:T(8,128)(2,1)S(1)} %copy-done.1, ...), custom_call_target="tpu_custom_call" | custom-call | flops 500000000 | bytes 1785856 | tf_op jit(solution)/shard_map/pallas_call | solution.py:192
  43.4 9.3 %all_to_all.16 = f32[4,128,128]{2,1,0:T(8,128)S(1)} all-to-all(f32[4,128,128]{2,1,0:T(8,128)S(1)} %bitcast.18), channel_id=1, replica_groups={{0,2,4,6},{1,3,5,7},{8,10,12,14},{9,11,13,15},{16,18,20,22},{17,19,21,2..., dimensions={0} | all-to-all | bytes 524288 | tf_op jit(solution)/shard_map/all_to_all | solution.py:207
  52.7 1.0 %shard_map.106 = f32[320,128]{1,0:T(8,128)S(1)} custom-call(f32[512,128]{1,0:T(8,128)S(1)} %bitcast.17, f32[256,256]{1,0:T(8,128)S(1)} %get-tuple-element.7.spec_ref, bf16[128,256]{1,0:T(8,128)(2,1)S(1)} %copy-done.3, bf16[64,384]{1,0:T(8,128)(2,1)S(1)} %copy-done.4, f32[2,64,128]{2,1,0:T(8,128)S(1)} %copy-done.2, bf16[768,256]{1,0:T(8,128)(2,1)S(1)} %copy-done.1, ...), custom_call_target="tpu_custom_call" | custom-call | flops 500000000 | bytes 1654784 | tf_op jit(solution)/shard_map/pallas_call | solution.py:192
  53.7 22.0 %all_to_all.17 = f32[64,5,1,128]{3,2,1,0:T(1,128)S(1)} all-to-all(f32[64,5,1,128]{3,2,1,0:T(1,128)S(1)} %bitcast.19), channel_id=1, replica_groups=mesh['seq'=64,'dp'=8] {'seq'}, dimensions={0} | all-to-all | bytes 327680 | tf_op jit(solution)/shard_map/all_to_all | solution.py:207
  75.7 6.2 %collective-permute-start = (f32[32,128]{1,0:T(8,128)S(1)}, f32[32,128]{1,0:T(8,128)S(1)}, u32[]{:S(2)}, u32[]{:S(2)}) collective-permute-start(f32[32,128]{1,0:T(8,128)S(1)} %get-tuple-element.9), channel_id=1, source_target_pairs={{0,1},{1,0},{2,3},{3,2},{4,5},{5,4},{6,7},{7,6},{8,9},{9,8},{10,11... | collective-permute-start | bytes 49160 | tf_op jit(solution)/shard_map/ppermute | solution.py:269
  82.0 0.7 shard_map.107
  82.7 0.1 collective-permute-done
  82.8 0.6 add_bitcast_fusion
  (1 shorter events, 0.0 us)
Async XLA Ops:
  0.6 41.5 %copy-start.1 = (bf16[768,256]{1,0:T(8,128)(2,1)S(1)}, bf16[768,256]{1,0:T(8,128)(2,1)}, u32[]{:S(2)}) copy-start(bf16[768,256]{1,0:T(8,128)(2,1)} %constant.22.clone.forward_ref) | copy-start | bytes 1179652
  2.6 39.5 %copy-start = (bf16[768,256]{1,0:T(8,128)(2,1)S(1)}, bf16[768,256]{1,0:T(8,128)(2,1)}, u32[]{:S(2)}) copy-start(bf16[768,256]{1,0:T(8,128)(2,1)} %constant.23.clone.inverse_ref) | copy-start | bytes 1179652
  2.6 39.5 %copy-start.2 = (f32[2,64,128]{2,1,0:T(8,128)S(1)}, f32[2,64,128]{2,1,0:T(8,128)}, u32[]{:S(2)}) copy-start(f32[2,64,128]{2,1,0:T(8,128)} %constant.21.clone.turn_ref) | copy-start | bytes 196612
  2.6 39.5 %copy-start.3 = (bf16[128,256]{1,0:T(8,128)(2,1)S(1)}, bf16[128,256]{1,0:T(8,128)(2,1)}, u32[]{:S(2)}) copy-start(bf16[128,256]{1,0:T(8,128)(2,1)} %constant.19.clone.first_ref) | copy-start | bytes 196612
  2.6 39.5 %copy-start.4 = (bf16[64,384]{1,0:T(8,128)(2,1)S(1)}, bf16[64,384]{1,0:T(8,128)(2,1)}, u32[]{:S(2)}) copy-start(bf16[64,384]{1,0:T(8,128)(2,1)} %constant.20.clone.last_ref) | copy-start | bytes 147460
  75.7 7.1 %collective-permute-start = (f32[32,128]{1,0:T(8,128)S(1)}, f32[32,128]{1,0:T(8,128)S(1)}, u32[]{:S(2)}, u32[]{:S(2)}) collective-permute-start(f32[32,128]{1,0:T(8,128)S(1)} %get-tuple-element.9), channel_id=1, source_target_pairs={{0,1},{1,0},{2,3},{3,2},{4,5},{5,4},{6,7},{7,6},{8,9},{9,8},{10,11... | collective-permute-start | bytes 49160 | tf_op jit(solution)/shard_map/ppermute | solution.py:269

commit v5 on v3

--- a/solution.py
+++ b/solution.py
@@ -60,26 +60,21 @@
     return jnp.dot(left, right, preferred_element_type=F32)
 
 
-def pack_kernel(own_ref, seat_ref, signal_hbm, grads_hbm, taps_hbm, gain_hbm, out_ref, signal_ref, grads_ref, taps_ref, gain_ref, turned, sems):
-    pairs = ((signal_hbm, signal_ref), (grads_hbm, grads_ref), (taps_hbm, taps_ref), (gain_hbm, gain_ref))
-    copies = [pltpu.make_async_copy(src, dst, sems.at[i]) for i, (src, dst) in enumerate(pairs)]
-    for copy in copies:
-        copy.start()
+def mask_kernel(seat_ref, out_ref):
+    out_ref[...] = jnp.where(seat_ref[0] == 0, jnp.ones(out_ref.shape, F32), jnp.zeros(out_ref.shape, F32))
+
+
+def pack_kernel(own_ref, mask_ref, signal_ref, grads_ref, taps_ref, gain_ref, out_ref, turned):
     for kind, ref in enumerate((signal_ref, grads_ref)):
-        copies[kind].wait()
         value = ref[...].astype(F32).T
         for block in range(2 * GROUP):
             odd, sub = divmod(block, GROUP)
             rows = value[BLOCK * block : BLOCK * (block + 1)]
             out_ref[pl.ds(SENT * odd + GROUP * kind + sub, BLOCK, stride=2 * SENT), :] = rows
-    copies[2].wait()
-    copies[3].wait()
-
-    @pl.when(seat_ref[0] == 0)
-    def _():
-        taps_ref[:1] = taps_ref[:1] + gain_ref[...]
-
-    turned[...] = taps_ref[...].T
+    taps = taps_ref[...]
+    first = lax.broadcasted_iota(jnp.int32, taps.shape, 0) == 0
+    taps = taps + jnp.where(first, gain_ref[...] * mask_ref[...], 0.0)
+    turned[...] = taps.T
     sub = own_ref[0] // 2
     for odd in range(2):
         start = pl.multiple_of(BLOCK * (GROUP * odd + sub), BLOCK)
@@ -187,12 +182,11 @@
     grad_ref[...] = jnp.where(odd == 0, load(0, GROUP), load(1, GROUP))
 
 
-def call(kernel, shapes, *args, flops=1000, scratch=(), hbm=False, scalars=0):
+def call(kernel, shapes, *args, flops=1000, scratch=(), scalars=0):
     outs = [jax.ShapeDtypeStruct(*one) for one in shapes]
     size = sum(math.prod(a.shape) * a.dtype.itemsize for a in [*args, *outs])
     vmem = pl.BlockSpec(memory_space=pltpu.VMEM)
-    place_in = pl.BlockSpec(memory_space=pltpu.HBM) if hbm else vmem
-    specs = [place_in] * len(args)
+    specs = [vmem] * len(args)
     specs[:scalars] = [pl.BlockSpec(memory_space=pltpu.SMEM)] * scalars
     result = pl.pallas_call(
         kernel,
@@ -201,7 +195,7 @@
         out_specs=[vmem] * len(outs),
         scratch_shapes=list(scratch),
         cost_estimate=pl.CostEstimate(flops=flops, bytes_accessed=size, transcendentals=0),
-        compiler_params=pltpu.CompilerParams(vmem_limit_bytes=58000000 if hbm else 24 * 1024 * 1024),
+        compiler_params=pltpu.CompilerParams(vmem_limit_bytes=24 * 1024 * 1024),
     )(*args)
     return result if len(shapes) > 1 else result[0]
 
@@ -228,25 +222,18 @@
             pltpu.VMEM((GROUP * HALF, wide), F32),
         )
 
+    mask = call(mask_kernel, [((1, chans), F32)], seat, flops=500_000_000, scalars=1)
     packed = call(
         pack_kernel,
         [((SENT * parts, rows), F32)],
         own,
-        seat,
+        mask,
         inputs[0],
         cotangent[0],
         filter_taps,
         skip_gain[None],
-        hbm=True,
-        scalars=2,
-        scratch=(
-            pltpu.VMEM((rows, chans), BF),
-            pltpu.VMEM((rows, chans), BF),
-            pltpu.VMEM((rows, chans), F32),
-            pltpu.VMEM((1, chans), F32),
-            pltpu.VMEM((chans, rows), F32),
-            pltpu.SemaphoreType.DMA((4,)),
-        ),
+        scalars=1,
+        scratch=(pltpu.VMEM((chans, rows), F32),),
     )
     columns = exchange(packed, "seq", (SENT, 1))
     spec, partial = call(

time: 82.9 us -> 81.8 us (0.987)
  Pallas kernels: 4.89 us -> 3.07 us
  local copies, waits for them, and re-layouts: 0.03 us -> 0.92 us
    pallas_call x4 -> x5, Pallas kernels: 4.89 us -> 3.07 us  [call(): pl.pallas_call(kernel, out_shape=outs, in_specs=specs, out_specs=[vmem] *...]
    unnamed x10 -> x18, local copies, waits for them, and re-layouts: 0.03 us -> 0.92 us
where the time goes in v5:
time: 81.8 us; the launch traced here: 80.4 us
  blocking collectives  75.6 us (92%)
  Pallas kernels  3.07 us (4%)
  local copies, waits for them, and re-layouts  0.92 us (1%)
    all_to_all x3, blocking collectives, exchange(): lax.all_to_all(blocks, axis, split_axis=0, concat_axis=0, tiled=True)  75.6 us
    pallas_call x5, Pallas kernels, call(): pl.pallas_call(kernel, out_shape=outs, in_specs=specs, out_specs=[vmem] *...  3.07 us

profile of v5, /device:TPU:1, one launch (start us, length us, event | category | flops | bytes accessed | tf_op | source)
XLA Modules:
  0.0 80.4 jit_solution(13903269760229127496)
XLA Ops:
  0.6 0.0 copy-start
  0.6 0.0 copy-start.1
  0.7 0.0 copy-start.2
  0.7 0.0 copy-start.3
  0.7 0.8 %copy-done = f32[128,256]{1,0:T(8,128)S(1)} copy-done((f32[128,256]{1,0:T(8,128)S(1)}, f32[128,256]{1,0:T(8,128)}, u32[]{:S(2)}) %copy-start) | copy-done | bytes 131096
  1.5 0.0 copy-done.1
  1.5 0.0 copy-done.2
  1.6 0.0 copy-done.3
  1.6 0.1 shard_map.105
  1.7 0.0 copy-start.4
  1.7 0.0 copy-start.6
  1.7 0.0 copy-start.7
  1.8 0.0 copy-start.8
  1.8 39.2 %all_to_all.15 = f32[64,9,1,128]{3,2,1,0:T(1,128)S(1)} all-to-all(f32[64,9,1,128]{3,2,1,0:T(1,128)S(1)} %bitcast.13), channel_id=1, replica_groups=mesh['seq'=64,'dp'=8] {'seq'}, dimensions={0} | all-to-all | bytes 589824 | tf_op jit(solution)/shard_map/all_to_all | solution.py:206
  41.0 0.0 copy-done.5
  41.0 0.0 copy-done.4
  41.0 0.0 copy-done.6
  41.0 0.0 copy-done.7
  41.0 0.0 copy-done.8
  41.0 1.2 %shard_map.106 = (f32[256,256]{1,0:T(8,128)S(1)}, f32[768,128]{1,0:T(8,128)S(1)}) custom-call(s32[1]{0:T(128)} %bitcast.own_ref, f32[576,128]{1,0:T(8,128)S(1)} %bitcast.17, bf16[128,256]{1,0:T(8,128)(2,1)S(1)} %copy-done.7, bf16[64,384]{1,0:T(8,128)(2,1)S(1)} %copy-done.8, f32[2,64,128]{2,1,0:T(8,128)S(1)} %copy-done.6, bf16[768,256]{1,0:T(8,128)(2,1)S(1)} %copy-done.5, ...), custom_call_target="tpu_custom_call" | custom-call | flops 500000000 | bytes 1916932 | tf_op jit(solution)/shard_map/pallas_call | solution.py:191
  42.3 15.4 %all_to_all.16 = f32[8,96,128]{2,1,0:T(8,128)S(1)} all-to-all(f32[8,96,128]{2,1,0:T(8,128)S(1)} %bitcast.16), channel_id=1, replica_groups=mesh['seq'=64,'dp'=8] {'dp'}, dimensions={0} | all-to-all | bytes 786432 | tf_op jit(solution)/shard_map/all_to_all | solution.py:206
  57.7 1.0 %shard_map.107 = f32[320,128]{1,0:T(8,128)S(1)} custom-call(f32[768,128]{1,0:T(8,128)S(1)} %bitcast.15, f32[256,256]{1,0:T(8,128)S(1)} %get-tuple-element.7.spec_ref, bf16[128,256]{1,0:T(8,128)(2,1)S(1)} %copy-done.7, bf16[64,384]{1,0:T(8,128)(2,1)S(1)} %copy-done.8, f32[2,64,128]{2,1,0:T(8,128)S(1)} %copy-done.6, bf16[768,256]{1,0:T(8,128)(2,1)S(1)} %copy-done.5, ...), custom_call_target="tpu_custom_call" | custom-call | flops 500000000 | bytes 1785856 | tf_op jit(solution)/shard_map/pallas_call | solution.py:191
  58.7 20.9 %all_to_all.17 = f32[64,5,1,128]{3,2,1,0:T(1,128)S(1)} all-to-all(f32[64,5,1,128]{3,2,1,0:T(1,128)S(1)} %bitcast.18), channel_id=1, replica_groups=mesh['seq'=64,'dp'=8] {'seq'}, dimensions={0} | all-to-all | bytes 327680 | tf_op jit(solution)/shard_map/all_to_all | solution.py:206
  79.6 0.7 shard_map.108
  (2 shorter events, 0.0 us)
Async XLA Ops:
  0.6 0.9 %copy-start = (f32[128,256]{1,0:T(8,128)S(1)}, f32[128,256]{1,0:T(8,128)}, u32[]{:S(2)}) copy-start(f32[128,256]{1,0:T(8,128)} %taps_ref.1) | copy-start | bytes 393220
  0.6 0.9 %copy-start.1 = (bf16[1,128,256]{2,1,0:T(8,128)(2,1)S(1)}, bf16[1,128,256]{2,1,0:T(8,128)(2,1)}, u32[]{:S(2)}) copy-start(bf16[1,128,256]{2,1,0:T(8,128)(2,1)} %param.9) | copy-start | bytes 196612
  0.7 0.9 %copy-start.2 = (bf16[1,128,256]{2,1,0:T(8,128)(2,1)S(1)}, bf16[1,128,256]{2,1,0:T(8,128)(2,1)}, u32[]{:S(2)}) copy-start(bf16[1,128,256]{2,1,0:T(8,128)(2,1)} %param.10) | copy-start | bytes 196612
  0.7 0.9 %copy-start.3 = (f32[256]{0:T(256)S(1)}, f32[256]{0:T(256)}, u32[]{:S(2)}) copy-start(f32[256]{0:T(256)} %param.12) | copy-start | bytes 3076
  1.6 39.4 %copy-start.5 = (bf16[768,256]{1,0:T(8,128)(2,1)S(1)}, bf16[768,256]{1,0:T(8,128)(2,1)}, u32[]{:S(2)}) copy-start(bf16[768,256]{1,0:T(8,128)(2,1)} %constant.22.clone.forward_ref) | copy-start | bytes 1179652
  1.7 39.3 %copy-start.4 = (bf16[768,256]{1,0:T(8,128)(2,1)S(1)}, bf16[768,256]{1,0:T(8,128)(2,1)}, u32[]{:S(2)}) copy-start(bf16[768,256]{1,0:T(8,128)(2,1)} %constant.23.clone.inverse_ref) | copy-start | bytes 1179652
  1.7 39.3 %copy-start.6 = (f32[2,64,128]{2,1,0:T(8,128)S(1)}, f32[2,64,128]{2,1,0:T(8,128)}, u32[]{:S(2)}) copy-start(f32[2,64,128]{2,1,0:T(8,128)} %constant.21.clone.turn_ref) | copy-start | bytes 196612
  1.7 39.3 %copy-start.7 = (bf16[128,256]{1,0:T(8,128)(2,1)S(1)}, bf16[128,256]{1,0:T(8,128)(2,1)}, u32[]{:S(2)}) copy-start(bf16[128,256]{1,0:T(8,128)(2,1)} %constant.19.clone.first_ref) | copy-start | bytes 196612
  1.8 39.3 %copy-start.8 = (bf16[64,384]{1,0:T(8,128)(2,1)S(1)}, bf16[64,384]{1,0:T(8,128)(2,1)}, u32[]{:S(2)}) copy-start(bf16[64,384]{1,0:T(8,128)(2,1)} %constant.20.clone.last_ref) | copy-start | bytes 147460

commit v6 on v5

--- a/solution.py
+++ b/solution.py
@@ -102,20 +102,17 @@
 
 def settle(back, last_ref, turn_ref):
     cosine, sine = turn_ref[0], turn_ref[1]
-    results = []
-    for index in range(0, GROUP, 2):
-        stacks = []
-        for one in (index, index + 1):
-            rows = pl.ds(HALF * one, HALF)
-            real, imag = back[rows, :SIDE], back[rows, SIDE:]
-            value = jnp.concatenate(
-                [real * cosine + imag * sine, imag * cosine - real * sine], axis=0
-            )
-            high, low = split(value)
-            stacks.append(jnp.concatenate([high, low, high], axis=0))
-        both = dot(last_ref[...], jnp.concatenate(stacks, axis=1))
-        results += [both[:, :SIDE], both[:, SIDE:]]
-    return results
+    stacks = []
+    for one in range(GROUP):
+        rows = pl.ds(HALF * one, HALF)
+        real, imag = back[rows, :SIDE], back[rows, SIDE:]
+        value = jnp.concatenate(
+            [real * cosine + imag * sine, imag * cosine - real * sine], axis=0
+        )
+        high, low = split(value)
+        stacks.append(jnp.concatenate([high, low, high], axis=0))
+    joined = dot(last_ref[...], jnp.concatenate(stacks, axis=1))
+    return [joined[:, SIDE * one : SIDE * (one + 1)] for one in range(GROUP)]
 
 
 def grad_kernel(own_ref, in_ref, first_ref, last_ref, turn_ref, forward_ref, inverse_ref, spec_ref, out_ref, spread, spectrum, mixed, back, taps):
@@ -123,11 +120,10 @@
         return in_ref[pl.ds(row, HALF, stride=SENT), :]
 
     taps[...] = load(2 * GROUP)
-    for sub in range(GROUP):
-        pair = jnp.concatenate([load(sub), load(GROUP + sub)], axis=1).astype(BF)
-        both = dot(first_ref[:, :SIDE], jnp.concatenate([pair, pair], axis=0))
-        place(spread, turn_ref, sub, both[:, :SIDE])
-        place(spread, turn_ref, GROUP + sub, both[:, SIDE:])
+    columns = jnp.concatenate([load(row) for row in range(2 * GROUP)], axis=1).astype(BF)
+    joined = dot(first_ref[:, :SIDE], jnp.concatenate([columns, columns], axis=0))
+    for index in range(2 * GROUP):
+        place(spread, turn_ref, index, joined[:, SIDE * index : SIDE * (index + 1)])
     spectrum[...] = wide_dot(spread, forward_ref)
     spec_ref[...] = spectrum[: GROUP * HALF]
     for sub in range(GROUP):
@@ -152,11 +148,10 @@
         starts = [MID * (2 * sub + core) + HALF for core in range(2)]
         return jnp.concatenate([in_ref[pl.ds(start, BLOCK), :] for start in starts], axis=0)
 
-    for sub in range(0, GROUP, 2):
-        high, low = split(jnp.concatenate([taps(sub), taps(sub + 1)], axis=1))
-        both = dot(first_ref[...], jnp.concatenate([high, high, low, low], axis=0))
-        place(spread, turn_ref, sub, both[:, :SIDE])
-        place(spread, turn_ref, sub + 1, both[:, SIDE:])
+    high, low = split(jnp.concatenate([taps(sub) for sub in range(GROUP)], axis=1))
+    joined = dot(first_ref[...], jnp.concatenate([high, high, low, low], axis=0))
+    for sub in range(GROUP):
+        place(spread, turn_ref, sub, joined[:, SIDE * sub : SIDE * (sub + 1)])
     spectrum[...] = wide_dot(spread, forward_ref)
     for sub in range(GROUP):
         rows = pl.ds(HALF * sub, HALF)

time: 81.8 us -> 81.7 us (level)
  no operation moved by 1% of the time
where the time goes in v6:
time: 81.7 us; the launch traced here: 80.3 us
  blocking collectives  75.6 us (93%)
  Pallas kernels  3 us (4%)
  local copies, waits for them, and re-layouts  0.92 us (1%)
    all_to_all x3, blocking collectives, exchange(): lax.all_to_all(blocks, axis, split_axis=0, concat_axis=0, tiled=True)  75.6 us
    pallas_call x5, Pallas kernels, call(): pl.pallas_call(kernel, out_shape=outs, in_specs=specs, out_specs=[vmem] *...  3 us

profile of v6, /device:TPU:1, one launch (start us, length us, event | category | flops | bytes accessed | tf_op | source)
XLA Modules:
  0.0 80.3 jit_solution(10204554444900015394)
XLA Ops:
  0.6 0.0 copy-start
  0.6 0.0 copy-start.1
  0.7 0.0 copy-start.2
  0.7 0.0 copy-start.3
  0.7 0.8 %copy-done = f32[128,256]{1,0:T(8,128)S(1)} copy-done((f32[128,256]{1,0:T(8,128)S(1)}, f32[128,256]{1,0:T(8,128)}, u32[]{:S(2)}) %copy-start) | copy-done | bytes 131096
  1.5 0.0 copy-done.1
  1.5 0.0 copy-done.2
  1.6 0.0 copy-done.3
  1.6 0.1 shard_map.105
  1.7 0.0 copy-start.4
  1.7 0.0 copy-start.6
  1.7 0.0 copy-start.7
  1.8 0.0 copy-start.8
  1.8 39.2 %all_to_all.15 = f32[64,9,1,128]{3,2,1,0:T(1,128)S(1)} all-to-all(f32[64,9,1,128]{3,2,1,0:T(1,128)S(1)} %bitcast.13), channel_id=1, replica_groups=mesh['seq'=64,'dp'=8] {'seq'}, dimensions={0} | all-to-all | bytes 589824 | tf_op jit(solution)/shard_map/all_to_all | solution.py:201
  41.0 0.0 copy-done.5
  41.0 0.0 copy-done.4
  41.0 0.0 copy-done.6
  41.0 0.0 copy-done.7
  41.0 0.0 copy-done.8
  41.0 1.1 %shard_map.106 = (f32[256,256]{1,0:T(8,128)S(1)}, f32[768,128]{1,0:T(8,128)S(1)}) custom-call(s32[1]{0:T(128)} %bitcast.own_ref, f32[576,128]{1,0:T(8,128)S(1)} %bitcast.17, bf16[128,256]{1,0:T(8,128)(2,1)S(1)} %copy-done.7, bf16[64,384]{1,0:T(8,128)(2,1)S(1)} %copy-done.8, f32[2,64,128]{2,1,0:T(8,128)S(1)} %copy-done.6, bf16[768,256]{1,0:T(8,128)(2,1)S(1)} %copy-done.5, ...), custom_call_target="tpu_custom_call" | custom-call | flops 500000000 | bytes 1916932 | tf_op jit(solution)/shard_map/pallas_call | solution.py:186
  42.2 15.4 %all_to_all.16 = f32[8,96,128]{2,1,0:T(8,128)S(1)} all-to-all(f32[8,96,128]{2,1,0:T(8,128)S(1)} %bitcast.16), channel_id=1, replica_groups=mesh['seq'=64,'dp'=8] {'dp'}, dimensions={0} | all-to-all | bytes 786432 | tf_op jit(solution)/shard_map/all_to_all | solution.py:201
  57.6 1.0 %shard_map.107 = f32[320,128]{1,0:T(8,128)S(1)} custom-call(f32[768,128]{1,0:T(8,128)S(1)} %bitcast.15, f32[256,256]{1,0:T(8,128)S(1)} %get-tuple-element.7.spec_ref, bf16[128,256]{1,0:T(8,128)(2,1)S(1)} %copy-done.7, bf16[64,384]{1,0:T(8,128)(2,1)S(1)} %copy-done.8, f32[2,64,128]{2,1,0:T(8,128)S(1)} %copy-done.6, bf16[768,256]{1,0:T(8,128)(2,1)S(1)} %copy-done.5, ...), custom_call_target="tpu_custom_call" | custom-call | flops 500000000 | bytes 1785856 | tf_op jit(solution)/shard_map/pallas_call | solution.py:186
  58.6 20.9 %all_to_all.17 = f32[64,5,1,128]{3,2,1,0:T(1,128)S(1)} all-to-all(f32[64,5,1,128]{3,2,1,0:T(1,128)S(1)} %bitcast.18), channel_id=1, replica_groups=mesh['seq'=64,'dp'=8] {'seq'}, dimensions={0} | all-to-all | bytes 327680 | tf_op jit(solution)/shard_map/all_to_all | solution.py:201
  79.6 0.7 shard_map.108
  (2 shorter events, 0.0 us)
Async XLA Ops:
  0.6 0.9 %copy-start = (f32[128,256]{1,0:T(8,128)S(1)}, f32[128,256]{1,0:T(8,128)}, u32[]{:S(2)}) copy-start(f32[128,256]{1,0:T(8,128)} %taps_ref.1) | copy-start | bytes 393220
  0.6 0.9 %copy-start.1 = (bf16[1,128,256]{2,1,0:T(8,128)(2,1)S(1)}, bf16[1,128,256]{2,1,0:T(8,128)(2,1)}, u32[]{:S(2)}) copy-start(bf16[1,128,256]{2,1,0:T(8,128)(2,1)} %param.9) | copy-start | bytes 196612
  0.7 0.9 %copy-start.2 = (bf16[1,128,256]{2,1,0:T(8,128)(2,1)S(1)}, bf16[1,128,256]{2,1,0:T(8,128)(2,1)}, u32[]{:S(2)}) copy-start(bf16[1,128,256]{2,1,0:T(8,128)(2,1)} %param.10) | copy-start | bytes 196612
  0.7 0.9 %copy-start.3 = (f32[256]{0:T(256)S(1)}, f32[256]{0:T(256)}, u32[]{:S(2)}) copy-start(f32[256]{0:T(256)} %param.12) | copy-start | bytes 3076
  1.6 39.4 %copy-start.5 = (bf16[768,256]{1,0:T(8,128)(2,1)S(1)}, bf16[768,256]{1,0:T(8,128)(2,1)}, u32[]{:S(2)}) copy-start(bf16[768,256]{1,0:T(8,128)(2,1)} %constant.22.clone.forward_ref) | copy-start | bytes 1179652
  1.7 39.3 %copy-start.4 = (bf16[768,256]{1,0:T(8,128)(2,1)S(1)}, bf16[768,256]{1,0:T(8,128)(2,1)}, u32[]{:S(2)}) copy-start(bf16[768,256]{1,0:T(8,128)(2,1)} %constant.23.clone.inverse_ref) | copy-start | bytes 1179652
  1.7 39.3 %copy-start.6 = (f32[2,64,128]{2,1,0:T(8,128)S(1)}, f32[2,64,128]{2,1,0:T(8,128)}, u32[]{:S(2)}) copy-start(f32[2,64,128]{2,1,0:T(8,128)} %constant.21.clone.turn_ref) | copy-start | bytes 196612
  1.7 39.3 %copy-start.7 = (bf16[128,256]{1,0:T(8,128)(2,1)S(1)}, bf16[128,256]{1,0:T(8,128)(2,1)}, u32[]{:S(2)}) copy-start(bf16[128,256]{1,0:T(8,128)(2,1)} %constant.19.clone.first_ref) | copy-start | bytes 196612
  1.8 39.3 %copy-start.8 = (bf16[64,384]{1,0:T(8,128)(2,1)S(1)}, bf16[64,384]{1,0:T(8,128)(2,1)}, u32[]{:S(2)}) copy-start(bf16[64,384]{1,0:T(8,128)(2,1)} %constant.20.clone.last_ref) | copy-start | bytes 147460

commit v7 on v6

--- a/solution.py
+++ b/solution.py
@@ -45,9 +45,9 @@
     forward = np.block([[cosine, -sine], [sine, cosine]])
     inverse = np.block([[cosine, sine], [-sine, cosine]])
     high, low = halves(forward)
-    forward = np.concatenate([high, high, low], axis=0)
+    forward = np.concatenate([high, low], axis=0)
     high, low = halves(inverse)
-    inverse = np.concatenate([high, high, low], axis=0)
+    inverse = np.concatenate([high, low], axis=0)
     return first_in, last_out, turn, forward, inverse
 
 
@@ -89,15 +89,18 @@
 
 
 def keep(ref, index, real, imag):
-    rows = pl.ds(HALF * index, HALF)
+    count = ref.shape[0] // 2
     for part, value in enumerate((real, imag)):
         high, low = split(value)
-        ref[rows, pl.ds(SIDE * part, SIDE)] = high
-        ref[rows, pl.ds(2 * SIDE + SIDE * part, SIDE)] = low
+        lanes = pl.ds(SIDE * part, SIDE)
+        ref[pl.ds(HALF * index, HALF), lanes] = high
+        ref[pl.ds(count + HALF * index, HALF), lanes] = low
 
 
 def wide_dot(ref, table_ref):
-    return dot(ref[...], table_ref[: 4 * SIDE]) + dot(ref[:, : 2 * SIDE], table_ref[4 * SIDE :])
+    count = ref.shape[0] // 2
+    joined = dot(ref[...], table_ref[: 2 * SIDE])
+    return joined[:count] + joined[count:] + dot(ref[:count], table_ref[2 * SIDE :])
 
 
 def settle(back, last_ref, turn_ref):
@@ -211,9 +214,9 @@
 
     def room(count):
         return (
-            pltpu.VMEM((count * GROUP * HALF, 2 * wide), BF),
+            pltpu.VMEM((2 * count * GROUP * HALF, wide), BF),
             pltpu.VMEM((count * GROUP * HALF, wide), F32),
-            pltpu.VMEM((GROUP * HALF, 2 * wide), BF),
+            pltpu.VMEM((2 * GROUP * HALF, wide), BF),
             pltpu.VMEM((GROUP * HALF, wide), F32),
         )
 

time: 81.7 us -> 81.7 us (level)
  no operation moved by 1% of the time
where the time goes in v7:
time: 81.7 us; the launch traced here: 80.3 us
  blocking collectives  75.6 us (93%)
  Pallas kernels  3 us (4%)
  local copies, waits for them, and re-layouts  0.92 us (1%)
    all_to_all x3, blocking collectives, exchange(): lax.all_to_all(blocks, axis, split_axis=0, concat_axis=0, tiled=True)  75.6 us
    pallas_call x5, Pallas kernels, call(): pl.pallas_call(kernel, out_shape=outs, in_specs=specs, out_specs=[vmem] *...  3 us

profile of v7, /device:TPU:1, one launch (start us, length us, event | category | flops | bytes accessed | tf_op | source)
XLA Modules:
  0.0 80.3 jit_solution(2841772868187550944)
XLA Ops:
  0.6 0.0 copy-start
  0.6 0.0 copy-start.1
  0.7 0.0 copy-start.2
  0.7 0.0 copy-start.3
  0.7 0.8 %copy-done = f32[128,256]{1,0:T(8,128)S(1)} copy-done((f32[128,256]{1,0:T(8,128)S(1)}, f32[128,256]{1,0:T(8,128)}, u32[]{:S(2)}) %copy-start) | copy-done | bytes 131096
  1.5 0.0 copy-done.1
  1.5 0.0 copy-done.2
  1.6 0.0 copy-done.3
  1.6 0.0 copy-start.7
  1.6 0.1 shard_map.105
  1.7 0.0 copy-start.4
  1.7 0.0 copy-start.5
  1.7 0.0 copy-start.6
  1.8 39.2 %all_to_all.15 = f32[64,9,1,128]{3,2,1,0:T(1,128)S(1)} all-to-all(f32[64,9,1,128]{3,2,1,0:T(1,128)S(1)} %bitcast.13), channel_id=1, replica_groups=mesh['seq'=64,'dp'=8] {'seq'}, dimensions={0} | all-to-all | bytes 589824 | tf_op jit(solution)/shard_map/all_to_all | solution.py:204
  41.0 0.0 copy-done.7
  41.0 0.0 copy-done.8
  41.0 0.0 copy-done.4
  41.0 0.0 copy-done.5
  41.0 0.0 copy-done.6
  41.0 1.1 %shard_map.106 = (f32[256,256]{1,0:T(8,128)S(1)}, f32[768,128]{1,0:T(8,128)S(1)}) custom-call(s32[1]{0:T(128)} %bitcast.own_ref, f32[576,128]{1,0:T(8,128)S(1)} %bitcast.17, bf16[128,256]{1,0:T(8,128)(2,1)S(1)} %copy-done.7, bf16[64,384]{1,0:T(8,128)(2,1)S(1)} %copy-done.8, f32[2,64,128]{2,1,0:T(8,128)S(1)} %copy-done.6, bf16[512,256]{1,0:T(8,128)(2,1)S(1)} %copy-done.5, ...), custom_call_target="tpu_custom_call" | custom-call | flops 500000000 | bytes 1654788 | tf_op jit(solution)/shard_map/pallas_call | solution.py:189
  42.2 15.4 %all_to_all.16 = f32[8,96,128]{2,1,0:T(8,128)S(1)} all-to-all(f32[8,96,128]{2,1,0:T(8,128)S(1)} %bitcast.16), channel_id=1, replica_groups=mesh['seq'=64,'dp'=8] {'dp'}, dimensions={0} | all-to-all | bytes 786432 | tf_op jit(solution)/shard_map/all_to_all | solution.py:204
  57.6 1.0 %shard_map.107 = f32[320,128]{1,0:T(8,128)S(1)} custom-call(f32[768,128]{1,0:T(8,128)S(1)} %bitcast.15, f32[256,256]{1,0:T(8,128)S(1)} %get-tuple-element.7.spec_ref, bf16[128,256]{1,0:T(8,128)(2,1)S(1)} %copy-done.7, bf16[64,384]{1,0:T(8,128)(2,1)S(1)} %copy-done.8, f32[2,64,128]{2,1,0:T(8,128)S(1)} %copy-done.6, bf16[512,256]{1,0:T(8,128)(2,1)S(1)} %copy-done.5, ...), custom_call_target="tpu_custom_call" | custom-call | flops 500000000 | bytes 1523712 | tf_op jit(solution)/shard_map/pallas_call | solution.py:189
  58.6 20.9 %all_to_all.17 = f32[64,5,1,128]{3,2,1,0:T(1,128)S(1)} all-to-all(f32[64,5,1,128]{3,2,1,0:T(1,128)S(1)} %bitcast.18), channel_id=1, replica_groups=mesh['seq'=64,'dp'=8] {'seq'}, dimensions={0} | all-to-all | bytes 327680 | tf_op jit(solution)/shard_map/all_to_all | solution.py:204
  79.5 0.7 shard_map.108
  (2 shorter events, 0.0 us)
Async XLA Ops:
  0.6 0.9 %copy-start = (f32[128,256]{1,0:T(8,128)S(1)}, f32[128,256]{1,0:T(8,128)}, u32[]{:S(2)}) copy-start(f32[128,256]{1,0:T(8,128)} %taps_ref.1) | copy-start | bytes 393220
  0.6 0.9 %copy-start.1 = (bf16[1,128,256]{2,1,0:T(8,128)(2,1)S(1)}, bf16[1,128,256]{2,1,0:T(8,128)(2,1)}, u32[]{:S(2)}) copy-start(bf16[1,128,256]{2,1,0:T(8,128)(2,1)} %param.9) | copy-start | bytes 196612
  0.7 0.9 %copy-start.2 = (bf16[1,128,256]{2,1,0:T(8,128)(2,1)S(1)}, bf16[1,128,256]{2,1,0:T(8,128)(2,1)}, u32[]{:S(2)}) copy-start(bf16[1,128,256]{2,1,0:T(8,128)(2,1)} %param.10) | copy-start | bytes 196612
  0.7 0.9 %copy-start.3 = (f32[256]{0:T(256)S(1)}, f32[256]{0:T(256)}, u32[]{:S(2)}) copy-start(f32[256]{0:T(256)} %param.12) | copy-start | bytes 3076
  1.6 39.4 %copy-start.7 = (bf16[128,256]{1,0:T(8,128)(2,1)S(1)}, bf16[128,256]{1,0:T(8,128)(2,1)}, u32[]{:S(2)}) copy-start(bf16[128,256]{1,0:T(8,128)(2,1)} %constant.19.clone.first_ref) | copy-start | bytes 196612
  1.6 39.4 %copy-start.8 = (bf16[64,384]{1,0:T(8,128)(2,1)S(1)}, bf16[64,384]{1,0:T(8,128)(2,1)}, u32[]{:S(2)}) copy-start(bf16[64,384]{1,0:T(8,128)(2,1)} %constant.20.clone.last_ref) | copy-start | bytes 147460
  1.7 39.3 %copy-start.4 = (bf16[512,256]{1,0:T(8,128)(2,1)S(1)}, bf16[512,256]{1,0:T(8,128)(2,1)}, u32[]{:S(2)}) copy-start(bf16[512,256]{1,0:T(8,128)(2,1)} %constant.23.clone.inverse_ref) | copy-start | bytes 786436
  1.7 39.3 %copy-start.5 = (bf16[512,256]{1,0:T(8,128)(2,1)S(1)}, bf16[512,256]{1,0:T(8,128)(2,1)}, u32[]{:S(2)}) copy-start(bf16[512,256]{1,0:T(8,128)(2,1)} %constant.22.clone.forward_ref) | copy-start | bytes 786436
  1.7 39.3 %copy-start.6 = (f32[2,64,128]{2,1,0:T(8,128)S(1)}, f32[2,64,128]{2,1,0:T(8,128)}, u32[]{:S(2)}) copy-start(f32[2,64,128]{2,1,0:T(8,128)} %constant.21.clone.turn_ref) | copy-start | bytes 196612

commit v8 on v7

--- a/solution.py
+++ b/solution.py
@@ -123,6 +123,10 @@
         return in_ref[pl.ds(row, HALF, stride=SENT), :]
 
     taps[...] = load(2 * GROUP)
+    start = pl.multiple_of(BLOCK * (own_ref[0] % 2), BLOCK)
+    half = taps[pl.ds(start, BLOCK), :]
+    for target in range(2 * GROUP):
+        out_ref[pl.ds(MID * target + HALF, BLOCK), :] = half
     columns = jnp.concatenate([load(row) for row in range(2 * GROUP)], axis=1).astype(BF)
     joined = dot(first_ref[:, :SIDE], jnp.concatenate([columns, columns], axis=0))
     for index in range(2 * GROUP):
@@ -140,10 +144,6 @@
     for sub, value in enumerate(settle(back, last_ref, turn_ref)):
         for target in range(sub, 2 * GROUP, GROUP):
             out_ref[pl.ds(MID * target, HALF), :] = value
-    start = pl.multiple_of(BLOCK * (own_ref[0] % 2), BLOCK)
-    half = taps[pl.ds(start, BLOCK), :]
-    for target in range(2 * GROUP):
-        out_ref[pl.ds(MID * target + HALF, BLOCK), :] = half
 
 
 def conv_kernel(in_ref, spec_ref, first_ref, last_ref, turn_ref, forward_ref, inverse_ref, out_ref, spread, spectrum, mixed, back):
@@ -151,6 +151,10 @@
         starts = [MID * (2 * sub + core) + HALF for core in range(2)]
         return jnp.concatenate([in_ref[pl.ds(start, BLOCK), :] for start in starts], axis=0)
 
+    total = in_ref[pl.ds(0, HALF), :]
+    for source in range(1, 2 * GROUP):
+        total = total + in_ref[pl.ds(MID * source, HALF), :]
+    out_ref[pl.ds(GROUP, HALF, stride=BACK), :] = total
     high, low = split(jnp.concatenate([taps(sub) for sub in range(GROUP)], axis=1))
     joined = dot(first_ref[...], jnp.concatenate([high, high, low, low], axis=0))
     for sub in range(GROUP):
@@ -164,10 +168,6 @@
     back[...] = wide_dot(mixed, inverse_ref)
     for sub, value in enumerate(settle(back, last_ref, turn_ref)):
         out_ref[pl.ds(sub, HALF, stride=BACK), :] = value
-    total = in_ref[pl.ds(0, HALF), :]
-    for source in range(1, 2 * GROUP):
-        total = total + in_ref[pl.ds(MID * source, HALF), :]
-    out_ref[pl.ds(GROUP, HALF, stride=BACK), :] = total
 
 
 def finish_kernel(own_ref, in_ref, out_ref, grad_ref):

time: 81.7 us -> 81.7 us (level)
  no operation moved by 1% of the time
where the time goes in v8:
time: 81.7 us; the launch traced here: 80.3 us
  blocking collectives  75.6 us (93%)
  Pallas kernels  3 us (4%)
  local copies, waits for them, and re-layouts  0.92 us (1%)
    all_to_all x3, blocking collectives, exchange(): lax.all_to_all(blocks, axis, split_axis=0, concat_axis=0, tiled=True)  75.6 us
    pallas_call x5, Pallas kernels, call(): pl.pallas_call(kernel, out_shape=outs, in_specs=specs, out_specs=[vmem] *...  3 us

profile of v8, /device:TPU:1, one launch (start us, length us, event | category | flops | bytes accessed | tf_op | source)
XLA Modules:
  0.0 80.3 jit_solution(8209520920945616876)
XLA Ops:
  0.6 0.0 copy-start
  0.6 0.0 copy-start.1
  0.7 0.0 copy-start.2
  0.7 0.0 copy-start.3
  0.7 0.8 %copy-done = f32[128,256]{1,0:T(8,128)S(1)} copy-done((f32[128,256]{1,0:T(8,128)S(1)}, f32[128,256]{1,0:T(8,128)}, u32[]{:S(2)}) %copy-start) | copy-done | bytes 131096
  1.5 0.0 copy-done.1
  1.5 0.0 copy-done.2
  1.6 0.0 copy-done.3
  1.6 0.0 copy-start.7
  1.6 0.1 shard_map.105
  1.7 0.0 copy-start.4
  1.7 0.0 copy-start.5
  1.7 0.0 copy-start.6
  1.8 39.2 %all_to_all.15 = f32[64,9,1,128]{3,2,1,0:T(1,128)S(1)} all-to-all(f32[64,9,1,128]{3,2,1,0:T(1,128)S(1)} %bitcast.13), channel_id=1, replica_groups=mesh['seq'=64,'dp'=8] {'seq'}, dimensions={0} | all-to-all | bytes 589824 | tf_op jit(solution)/shard_map/all_to_all | solution.py:204
  41.0 0.0 copy-done.7
  41.0 0.0 copy-done.8
  41.0 0.0 copy-done.4
  41.0 0.0 copy-done.5
  41.0 0.0 copy-done.6
  41.0 1.1 %shard_map.106 = (f32[256,256]{1,0:T(8,128)S(1)}, f32[768,128]{1,0:T(8,128)S(1)}) custom-call(s32[1]{0:T(128)} %bitcast.own_ref, f32[576,128]{1,0:T(8,128)S(1)} %bitcast.17, bf16[128,256]{1,0:T(8,128)(2,1)S(1)} %copy-done.7, bf16[64,384]{1,0:T(8,128)(2,1)S(1)} %copy-done.8, f32[2,64,128]{2,1,0:T(8,128)S(1)} %copy-done.6, bf16[512,256]{1,0:T(8,128)(2,1)S(1)} %copy-done.5, ...), custom_call_target="tpu_custom_call" | custom-call | flops 500000000 | bytes 1654788 | tf_op jit(solution)/shard_map/pallas_call | solution.py:189
  42.2 15.4 %all_to_all.16 = f32[8,96,128]{2,1,0:T(8,128)S(1)} all-to-all(f32[8,96,128]{2,1,0:T(8,128)S(1)} %bitcast.16), channel_id=1, replica_groups=mesh['seq'=64,'dp'=8] {'dp'}, dimensions={0} | all-to-all | bytes 786432 | tf_op jit(solution)/shard_map/all_to_all | solution.py:204
  57.6 1.0 %shard_map.107 = f32[320,128]{1,0:T(8,128)S(1)} custom-call(f32[768,128]{1,0:T(8,128)S(1)} %bitcast.15, f32[256,256]{1,0:T(8,128)S(1)} %get-tuple-element.7.spec_ref, bf16[128,256]{1,0:T(8,128)(2,1)S(1)} %copy-done.7, bf16[64,384]{1,0:T(8,128)(2,1)S(1)} %copy-done.8, f32[2,64,128]{2,1,0:T(8,128)S(1)} %copy-done.6, bf16[512,256]{1,0:T(8,128)(2,1)S(1)} %copy-done.5, ...), custom_call_target="tpu_custom_call" | custom-call | flops 500000000 | bytes 1523712 | tf_op jit(solution)/shard_map/pallas_call | solution.py:189
  58.6 20.9 %all_to_all.17 = f32[64,5,1,128]{3,2,1,0:T(1,128)S(1)} all-to-all(f32[64,5,1,128]{3,2,1,0:T(1,128)S(1)} %bitcast.18), channel_id=1, replica_groups=mesh['seq'=64,'dp'=8] {'seq'}, dimensions={0} | all-to-all | bytes 327680 | tf_op jit(solution)/shard_map/all_to_all | solution.py:204
  79.5 0.7 shard_map.108
  (2 shorter events, 0.0 us)
Async XLA Ops:
  0.6 0.9 %copy-start = (f32[128,256]{1,0:T(8,128)S(1)}, f32[128,256]{1,0:T(8,128)}, u32[]{:S(2)}) copy-start(f32[128,256]{1,0:T(8,128)} %taps_ref.1) | copy-start | bytes 393220
  0.6 0.9 %copy-start.1 = (bf16[1,128,256]{2,1,0:T(8,128)(2,1)S(1)}, bf16[1,128,256]{2,1,0:T(8,128)(2,1)}, u32[]{:S(2)}) copy-start(bf16[1,128,256]{2,1,0:T(8,128)(2,1)} %param.9) | copy-start | bytes 196612
  0.7 0.9 %copy-start.2 = (bf16[1,128,256]{2,1,0:T(8,128)(2,1)S(1)}, bf16[1,128,256]{2,1,0:T(8,128)(2,1)}, u32[]{:S(2)}) copy-start(bf16[1,128,256]{2,1,0:T(8,128)(2,1)} %param.10) | copy-start | bytes 196612
  0.7 0.9 %copy-start.3 = (f32[256]{0:T(256)S(1)}, f32[256]{0:T(256)}, u32[]{:S(2)}) copy-start(f32[256]{0:T(256)} %param.12) | copy-start | bytes 3076
  1.6 39.4 %copy-start.7 = (bf16[128,256]{1,0:T(8,128)(2,1)S(1)}, bf16[128,256]{1,0:T(8,128)(2,1)}, u32[]{:S(2)}) copy-start(bf16[128,256]{1,0:T(8,128)(2,1)} %constant.19.clone.first_ref) | copy-start | bytes 196612
  1.6 39.4 %copy-start.8 = (bf16[64,384]{1,0:T(8,128)(2,1)S(1)}, bf16[64,384]{1,0:T(8,128)(2,1)}, u32[]{:S(2)}) copy-start(bf16[64,384]{1,0:T(8,128)(2,1)} %constant.20.clone.last_ref) | copy-start | bytes 147460
  1.7 39.3 %copy-start.4 = (bf16[512,256]{1,0:T(8,128)(2,1)S(1)}, bf16[512,256]{1,0:T(8,128)(2,1)}, u32[]{:S(2)}) copy-start(bf16[512,256]{1,0:T(8,128)(2,1)} %constant.23.clone.inverse_ref) | copy-start | bytes 786436
  1.7 39.3 %copy-start.5 = (bf16[512,256]{1,0:T(8,128)(2,1)S(1)}, bf16[512,256]{1,0:T(8,128)(2,1)}, u32[]{:S(2)}) copy-start(bf16[512,256]{1,0:T(8,128)(2,1)} %constant.22.clone.forward_ref) | copy-start | bytes 786436
  1.7 39.3 %copy-start.6 = (f32[2,64,128]{2,1,0:T(8,128)S(1)}, f32[2,64,128]{2,1,0:T(8,128)}, u32[]{:S(2)}) copy-start(f32[2,64,128]{2,1,0:T(8,128)} %constant.21.clone.turn_ref) | copy-start | bytes 196612

commit v9 on v8

--- a/solution.py
+++ b/solution.py
@@ -123,10 +123,6 @@
         return in_ref[pl.ds(row, HALF, stride=SENT), :]
 
     taps[...] = load(2 * GROUP)
-    start = pl.multiple_of(BLOCK * (own_ref[0] % 2), BLOCK)
-    half = taps[pl.ds(start, BLOCK), :]
-    for target in range(2 * GROUP):
-        out_ref[pl.ds(MID * target + HALF, BLOCK), :] = half
     columns = jnp.concatenate([load(row) for row in range(2 * GROUP)], axis=1).astype(BF)
     joined = dot(first_ref[:, :SIDE], jnp.concatenate([columns, columns], axis=0))
     for index in range(2 * GROUP):
@@ -144,6 +140,10 @@
     for sub, value in enumerate(settle(back, last_ref, turn_ref)):
         for target in range(sub, 2 * GROUP, GROUP):
             out_ref[pl.ds(MID * target, HALF), :] = value
+    start = pl.multiple_of(BLOCK * (own_ref[0] % 2), BLOCK)
+    half = taps[pl.ds(start, BLOCK), :]
+    for target in range(2 * GROUP):
+        out_ref[pl.ds(MID * target + HALF, BLOCK), :] = half
 
 
 def conv_kernel(in_ref, spec_ref, first_ref, last_ref, turn_ref, forward_ref, inverse_ref, out_ref, spread, spectrum, mixed, back):

time: 81.7 us -> 81.7 us (level)
  no operation moved by 1% of the time
where the time goes in v9:
time: 81.7 us; the launch traced here: 80.3 us
  blocking collectives  75.6 us (93%)
  Pallas kernels  3 us (4%)
  local copies, waits for them, and re-layouts  0.92 us (1%)
    all_to_all x3, blocking collectives, exchange(): lax.all_to_all(blocks, axis, split_axis=0, concat_axis=0, tiled=True)  75.6 us
    pallas_call x5, Pallas kernels, call(): pl.pallas_call(kernel, out_shape=outs, in_specs=specs, out_specs=[vmem] *...  3 us

profile of v9, /device:TPU:1, one launch (start us, length us, event | category | flops | bytes accessed | tf_op | source)
XLA Modules:
  0.0 80.3 jit_solution(2807444999184566433)
XLA Ops:
  0.6 0.0 copy-start
  0.6 0.0 copy-start.1
  0.7 0.0 copy-start.2
  0.7 0.0 copy-start.3
  0.7 0.8 %copy-done = f32[128,256]{1,0:T(8,128)S(1)} copy-done((f32[128,256]{1,0:T(8,128)S(1)}, f32[128,256]{1,0:T(8,128)}, u32[]{:S(2)}) %copy-start) | copy-done | bytes 131096
  1.5 0.0 copy-done.1
  1.5 0.0 copy-done.2
  1.6 0.0 copy-done.3
  1.6 0.0 copy-start.7
  1.6 0.1 shard_map.105
  1.7 0.0 copy-start.4
  1.7 0.0 copy-start.5
  1.7 0.0 copy-start.6
  1.8 39.2 %all_to_all.15 = f32[64,9,1,128]{3,2,1,0:T(1,128)S(1)} all-to-all(f32[64,9,1,128]{3,2,1,0:T(1,128)S(1)} %bitcast.13), channel_id=1, replica_groups=mesh['seq'=64,'dp'=8] {'seq'}, dimensions={0} | all-to-all | bytes 589824 | tf_op jit(solution)/shard_map/all_to_all | solution.py:204
  41.0 0.0 copy-done.7
  41.0 0.0 copy-done.8
  41.0 0.0 copy-done.4
  41.0 0.0 copy-done.5
  41.0 0.0 copy-done.6
  41.0 1.1 %shard_map.106 = (f32[256,256]{1,0:T(8,128)S(1)}, f32[768,128]{1,0:T(8,128)S(1)}) custom-call(s32[1]{0:T(128)} %bitcast.own_ref, f32[576,128]{1,0:T(8,128)S(1)} %bitcast.17, bf16[128,256]{1,0:T(8,128)(2,1)S(1)} %copy-done.7, bf16[64,384]{1,0:T(8,128)(2,1)S(1)} %copy-done.8, f32[2,64,128]{2,1,0:T(8,128)S(1)} %copy-done.6, bf16[512,256]{1,0:T(8,128)(2,1)S(1)} %copy-done.5, ...), custom_call_target="tpu_custom_call" | custom-call | flops 500000000 | bytes 1654788 | tf_op jit(solution)/shard_map/pallas_call | solution.py:189
  42.2 15.4 %all_to_all.16 = f32[8,96,128]{2,1,0:T(8,128)S(1)} all-to-all(f32[8,96,128]{2,1,0:T(8,128)S(1)} %bitcast.16), channel_id=1, replica_groups=mesh['seq'=64,'dp'=8] {'dp'}, dimensions={0} | all-to-all | bytes 786432 | tf_op jit(solution)/shard_map/all_to_all | solution.py:204
  57.6 1.0 %shard_map.107 = f32[320,128]{1,0:T(8,128)S(1)} custom-call(f32[768,128]{1,0:T(8,128)S(1)} %bitcast.15, f32[256,256]{1,0:T(8,128)S(1)} %get-tuple-element.7.spec_ref, bf16[128,256]{1,0:T(8,128)(2,1)S(1)} %copy-done.7, bf16[64,384]{1,0:T(8,128)(2,1)S(1)} %copy-done.8, f32[2,64,128]{2,1,0:T(8,128)S(1)} %copy-done.6, bf16[512,256]{1,0:T(8,128)(2,1)S(1)} %copy-done.5, ...), custom_call_target="tpu_custom_call" | custom-call | flops 500000000 | bytes 1523712 | tf_op jit(solution)/shard_map/pallas_call | solution.py:189
  58.6 20.9 %all_to_all.17 = f32[64,5,1,128]{3,2,1,0:T(1,128)S(1)} all-to-all(f32[64,5,1,128]{3,2,1,0:T(1,128)S(1)} %bitcast.18), channel_id=1, replica_groups=mesh['seq'=64,'dp'=8] {'seq'}, dimensions={0} | all-to-all | bytes 327680 | tf_op jit(solution)/shard_map/all_to_all | solution.py:204
  79.5 0.7 shard_map.108
  (2 shorter events, 0.0 us)
Async XLA Ops:
  0.6 0.9 %copy-start = (f32[128,256]{1,0:T(8,128)S(1)}, f32[128,256]{1,0:T(8,128)}, u32[]{:S(2)}) copy-start(f32[128,256]{1,0:T(8,128)} %taps_ref.1) | copy-start | bytes 393220
  0.6 0.9 %copy-start.1 = (bf16[1,128,256]{2,1,0:T(8,128)(2,1)S(1)}, bf16[1,128,256]{2,1,0:T(8,128)(2,1)}, u32[]{:S(2)}) copy-start(bf16[1,128,256]{2,1,0:T(8,128)(2,1)} %param.9) | copy-start | bytes 196612
  0.7 0.9 %copy-start.2 = (bf16[1,128,256]{2,1,0:T(8,128)(2,1)S(1)}, bf16[1,128,256]{2,1,0:T(8,128)(2,1)}, u32[]{:S(2)}) copy-start(bf16[1,128,256]{2,1,0:T(8,128)(2,1)} %param.10) | copy-start | bytes 196612
  0.7 0.9 %copy-start.3 = (f32[256]{0:T(256)S(1)}, f32[256]{0:T(256)}, u32[]{:S(2)}) copy-start(f32[256]{0:T(256)} %param.12) | copy-start | bytes 3076
  1.6 39.4 %copy-start.7 = (bf16[128,256]{1,0:T(8,128)(2,1)S(1)}, bf16[128,256]{1,0:T(8,128)(2,1)}, u32[]{:S(2)}) copy-start(bf16[128,256]{1,0:T(8,128)(2,1)} %constant.19.clone.first_ref) | copy-start | bytes 196612
  1.6 39.4 %copy-start.8 = (bf16[64,384]{1,0:T(8,128)(2,1)S(1)}, bf16[64,384]{1,0:T(8,128)(2,1)}, u32[]{:S(2)}) copy-start(bf16[64,384]{1,0:T(8,128)(2,1)} %constant.20.clone.last_ref) | copy-start | bytes 147460
  1.7 39.3 %copy-start.4 = (bf16[512,256]{1,0:T(8,128)(2,1)S(1)}, bf16[512,256]{1,0:T(8,128)(2,1)}, u32[]{:S(2)}) copy-start(bf16[512,256]{1,0:T(8,128)(2,1)} %constant.23.clone.inverse_ref) | copy-start | bytes 786436
  1.7 39.3 %copy-start.5 = (bf16[512,256]{1,0:T(8,128)(2,1)S(1)}, bf16[512,256]{1,0:T(8,128)(2,1)}, u32[]{:S(2)}) copy-start(bf16[512,256]{1,0:T(8,128)(2,1)} %constant.22.clone.forward_ref) | copy-start | bytes 786436
  1.7 39.3 %copy-start.6 = (f32[2,64,128]{2,1,0:T(8,128)S(1)}, f32[2,64,128]{2,1,0:T(8,128)}, u32[]{:S(2)}) copy-start(f32[2,64,128]{2,1,0:T(8,128)} %constant.21.clone.turn_ref) | copy-start | bytes 196612
